TPU v7x, 512 devices: a whole 4x8x8 slice. The times are simulated.
512 devices in a mesh: attn: 4 (over x), grp: 4 (over z_hi), exp: 32 (over z_lo, y, core).
Axes of the slice: x: 4, y: 8, z: 8 (z_hi: 4, z_lo: 2; z = z_hi * 2 + z_lo), core: 2. Of those that a mesh axis runs over, the one named last changes fastest.
Arguments:
- resid: bfloat16 [2, 128, 3584], P(None, 'grp'), may hold values from -36 to 36
- queries: bfloat16 [2, 128, 64, 576], P(None, ('grp', 'exp')), may hold values from -49 to 49
- cache: bfloat16 [2, 128, 2048, 576], P(None, ('grp', 'exp'), 'attn'), may hold values from -4 to 4
- lengths: int32 [2, 128], P(None, ('grp', 'exp')), may hold values from 2 to 2048, as said below
- w_value: bfloat16 [64, 512, 128], P('exp', None, 'attn'), may hold values from -2 to 2
- w_out: bfloat16 [64, 128, 3584], P('exp', 'attn'), may hold values from -0.0625 to 0.0625
- norm_gain: bfloat16 [3584], replicated, may hold values from 0.099609375 to 1.8984375
- route_ids: int32 [2, 128, 8], replicated, may hold values from 0 to 31, all different within a row; in each aligned block of 32 rows (0 to 31, 32 to 63, ..., all dimensions but the last counted through in order) at most 16 rows name the same one
- route_weights: float32 [2, 128, 8], replicated, may hold values from 0.05 to 1
- w_gate: bfloat16 [32, 3584, 2048], P('exp', None, ('attn', 'grp')), may hold values from -0.09375 to 0.09375
- w_up: bfloat16 [32, 3584, 2048], P('exp', None, ('attn', 'grp')), may hold values from -0.09375 to 0.09375
- w_down: bfloat16 [32, 2048, 3584], P('exp', ('attn', 'grp')), may hold values from -0.125 to 0.125
Outputs:
- layer_out: bfloat16 [2, 128, 3584], P(None, ('grp', 'exp'), 'attn')
Inputs may be any that keep to these rules, and one draw needn't show every extreme that they name: `route_ids`: each row names 8 different experts; among the 32 tokens of one group in one micro-batch (aligned blocks of rows) no expert is named more than 16 times, a bound that some block reaches. `lengths`: each micro-batch has a request of length 2048.
All inputs are finite; a program needn't handle non-finite values.
Results may differ from a plain program's by a relative error of at most 0.018.
Values may be sent and summed in bfloat16 or wider, within the bound.
A program may use at most 64 MiB of HBM per device.

v0:
```python
import jax
import jax.numpy as jnp
from jax import lax
from jax.sharding import PartitionSpec as P

ROPE = 64
V = 128
MB = 2


def normalize(hidden, norm_gain):
    mean_square = jnp.mean(hidden * hidden, axis=-1, keepdims=True)
    return hidden * lax.rsqrt(mean_square + 1e-06) * norm_gain.astype(jnp.float32)


def body(
    resid,
    queries,
    cache,
    lengths,
    w_value,
    w_out,
    norm_gain,
    route_ids,
    route_weights,
    w_gate,
    w_up,
    w_down,
):
    attn_count = lax.axis_size("attn")
    grp_count = lax.axis_size("grp")
    exp_count = lax.axis_size("exp")
    attn_index = lax.axis_index("attn")
    grp_index = lax.axis_index("grp")
    exp_index = lax.axis_index("exp")
    ctx_local = cache.shape[2]
    latent_width = w_value.shape[1]
    model_width = resid.shape[-1]
    quarter = model_width // attn_count
    route_count = route_ids.shape[2]
    capacity = 2 * route_count
    score_scale = (V + ROPE) ** (-0.5)
    positions = attn_index * ctx_local + jnp.arange(ctx_local, dtype=jnp.int32)
    results = []
    for micro_idx in range(MB):
        query_rows = queries[micro_idx, 0]
        key_rows = cache[micro_idx, 0]
        scores = (
            jnp.einsum("hk,pk->hp", query_rows, key_rows, preferred_element_type=jnp.float32)
            * score_scale
        )
        visible = positions[None, :] < lengths[micro_idx, 0]
        local_top = jnp.max(jnp.where(visible, scores, -1e30), axis=1)
        soft_weights = jnp.where(visible, jnp.exp(scores - local_top[:, None]), 0.0)
        local_total = jnp.sum(soft_weights, axis=1)
        local_acc = jnp.dot(
            soft_weights.astype(jnp.bfloat16),
            key_rows[:, :latent_width],
            preferred_element_type=jnp.float32,
        )
        row_top = lax.pmax(local_top, "attn")
        factor = jnp.exp(local_top - row_top)
        row_total, row_acc = (
            lax.psum((local_total * factor).astype(jnp.bfloat16), "attn").astype(jnp.float32),
            lax.psum((local_acc * factor[:, None]).astype(jnp.bfloat16), "attn").astype(
                jnp.float32
            ),
        )
        context = (row_acc / row_total[:, None]).astype(jnp.bfloat16)
        head_rows = lax.all_to_all(context[None], "exp", split_axis=1, concat_axis=0, tiled=True)
        values = jnp.einsum(
            "rhl,hlv->rhv", head_rows, w_value, preferred_element_type=jnp.float32
        ).astype(jnp.bfloat16)
        partial_out = jnp.einsum("rhv,hvd->rd", values, w_out, preferred_element_type=jnp.float32)
        attended = lax.psum(partial_out, ("attn", "exp"))
        hidden = resid[micro_idx].astype(jnp.float32) + attended
        normed = normalize(hidden, norm_gain).astype(jnp.bfloat16)
        group_ids = route_ids[micro_idx].reshape(grp_count, exp_count, route_count)
        group_wts = route_weights[micro_idx].reshape(grp_count, exp_count, route_count)
        matches = group_ids == exp_index
        routed = jnp.any(matches, axis=2).astype(jnp.int32)
        weight = jnp.sum(jnp.where(matches, group_wts, 0.0), axis=2)
        slot_index = jnp.cumsum(routed, axis=1) - routed
        choose = (
            slot_index[:, None, :] == jnp.arange(capacity, dtype=jnp.int32)[None, :, None]
        ) & (routed[:, None, :] > 0)
        choose_bf = choose.astype(jnp.bfloat16)
        own_choose = lax.dynamic_index_in_dim(choose_bf, grp_index, 0, keepdims=False)
        picked = jnp.dot(own_choose, normed, preferred_element_type=jnp.float32).astype(
            jnp.bfloat16
        )
        piece_rows = lax.all_gather(picked, "grp", axis=0, tiled=True)
        gate_proj = jnp.dot(piece_rows, w_gate[0], preferred_element_type=jnp.float32)
        up_proj = jnp.dot(piece_rows, w_up[0], preferred_element_type=jnp.float32)
        activation = (jax.nn.silu(gate_proj) * up_proj).astype(jnp.bfloat16)
        partial_down = jnp.dot(activation, w_down[0], preferred_element_type=jnp.float32)
        scaled = choose.astype(jnp.float32) * weight[:, None, :]
        own_sums = lax.psum_scatter(
            partial_down.reshape(grp_count, capacity, model_width).astype(jnp.bfloat16),
            "grp",
            scatter_dimension=0,
            tiled=True,
        ).astype(jnp.float32)
        own_scaled = lax.dynamic_index_in_dim(scaled, grp_index, 0, keepdims=False)
        spread = jnp.einsum(
            "ct,cad->atd",
            own_scaled,
            own_sums[0].reshape(capacity, attn_count, quarter),
            precision=lax.Precision.HIGHEST,
        )
        mixed = lax.psum_scatter(
            spread.reshape(attn_count * exp_count, quarter),
            ("attn", "exp"),
            scatter_dimension=0,
            tiled=True,
        )
        own_hidden = lax.dynamic_slice(hidden, (exp_index, attn_index * quarter), (1, quarter))
        results.append((own_hidden + mixed).astype(jnp.bfloat16))
    return jnp.stack(results)


def solution(mesh):
    return jax.shard_map(
        body,
        mesh=mesh,
        in_specs=(
            P(None, "grp", None),
            P(None, ("grp", "exp"), None, None),
            P(None, ("grp", "exp"), "attn", None),
            P(None, ("grp", "exp")),
            P("exp", None, "attn"),
            P("exp", "attn", None),
            P(),
            P(),
            P(),
            P("exp", None, ("attn", "grp")),
            P("exp", None, ("attn", "grp")),
            P("exp", ("attn", "grp"), None),
        ),
        out_specs=P(None, ("grp", "exp"), "attn"),
        check_vma=False,
    )
```

profile of v0, /device:TPU:1, one launch (start us, length us, event | category | flops | bytes accessed | tf_op | source)
XLA Modules:
  0.0 2326.2 jit_solution(8101633450826134530)
XLA Ops:
  6.5 1.4 fusion.77
  8.0 1.4 slice_bitcast_fusion.1
  9.4 1.3 fusion.66
  10.7 1.2 select_reduce_fusion.1
  12.0 1.2 select_reduce_fusion
  13.2 0.2 fusion.24
  13.4 9.3 all-reduce.4
  22.7 0.2 fusion.26
  22.9 0.9 fusion
  23.8 0.9 fusion.1
  24.8 6.0 all-reduce.5
  30.8 48.5 %all-reduce.15.cloned.1.call-done = (bf16[64,512]{1,0:T(8,128)(2,1)}, bf16[64,512]{1,0:T(8,128)(2,1)}) async-done(((bf16[64,512]{1,0:T(8,128)(2,1)}, bf16[64,512]{1,0:T(8,128)(2,1)}), (bf16[64,512]{1,0:T(8,128)(2,1)}, bf16[64,512]{1,0:T(8,128)(2,1)})) %all-reduce.15.cloned.1.call-update) | async-done | bytes 131088 | tf_op jit(solution)/shard_map/psum | solution.py:65
  79.4 0.9 fusion.34
  80.3 0.1 copy.40
  80.4 0.5 broadcast.106
  80.9 1.0 reduce.9
  81.9 0.6 reshape.128
  82.6 10.7 all-to-all-start
  93.3 0.9 fusion.35
  94.2 0.1 copy.39
  94.3 1.0 reduce.8
  95.4 0.7 reshape.126
  96.0 5.4 all-to-all-done
  101.4 4.8 all-to-all-start.1
  106.1 0.0 all-reduce.13.cloned.1.call-start
  106.2 0.1 reshape.129
  106.2 0.4 bitcast_reduce_fusion
  106.7 7.7 all-to-all-done.1
  114.3 0.1 reshape.127
  114.4 0.4 bitcast_reduce_fusion.1
  114.8 1.2 convolution_bitcast_fusion.1
  116.0 1.2 convolution_bitcast_fusion
  117.2 0.0 reduce-scatter.3.cloned.1.call-start
  117.3 0.1 reshape.114
  117.4 0.2 reduce_window_sum.17
  117.6 0.1 reshape.116
  117.7 0.2 reduce_window_sum.18
  118.0 1058.1 %all-reduce.13.cloned.1.call-done = (f32[32,3584]{1,0:T(8,128)}, f32[32,3584]{1,0:T(8,128)}) async-done(((f32[32,3584]{1,0:T(8,128)}, f32[32,3584]{1,0:T(8,128)}), (f32[32,3584]{1,0:T(8,128)}, f32[32,3584]{1,0:T(8,128)})) %all-reduce.13.cloned.1.call-update) | async-done | bytes 917520 | tf_op jit(solution)/shard_map/psum | solution.py:75
  1176.1 1.5 multiply_reduce_fusion.1
  1177.6 0.2 convolution_convert_fusion.3
  1177.8 14.6 all_gather.6
  1192.5 0.3 fusion.12
  1192.8 0.3 fusion.2
  1193.1 1.1 convolution_convert_fusion.1
  1194.2 0.0 reduce-scatter.5.cloned.1.call-start
  1194.3 0.2 convolution_convert_fusion.2
  1194.5 11.6 all_gather.7
  1206.1 0.3 fusion.10
  1206.4 0.3 fusion.3
  1206.7 1.1 convolution_convert_fusion
  1207.8 0.0 all-reduce.11.cloned.1.call-start
  1207.8 0.1 mul.117
  1207.9 0.1 mul.130
  1208.0 10.5 reduce-scatter.3.cloned.1.call-done
  1218.6 0.9 reshape_squeeze.4
  1219.5 1.2 fusion.22
  1220.7 29.1 %reduce-scatter.5.cloned.1.call-done = bf16[1,16,3584]{2,1,0:T(8,128)(2,1)} async-done(((bf16[4,16,3584]{2,1,0:T(8,128)(2,1)}), bf16[1,16,3584]{2,1,0:T(8,128)(2,1)}) %reduce-scatter.5.cloned.1.call-update) | async-done | bytes 114704 | tf_op jit(solution)/shard_map/reduce_scatter | solution.py:98
  1249.8 0.9 reshape_squeeze.5
  1250.7 1.2 fusion.20
  1251.9 1.3 dynamic-slice
  1253.2 1063.0 %all-reduce.11.cloned.1.call-done = (f32[128,896]{1,0:T(8,128)}, f32[128,896]{1,0:T(8,128)}) async-done(((f32[128,896]{1,0:T(8,128)}, f32[128,896]{1,0:T(8,128)}), (f32[128,896]{1,0:T(8,128)}, f32[128,896]{1,0:T(8,128)})) %all-reduce.11.cloned.1.call-update) | async-done | bytes 917520
  2316.2 1.5 fusion.65
  2317.6 1.5 fusion.63
  2319.1 0.6 pad_maximum_fusion
  (50 shorter events, 0.4 us)
Async XLA Ops:
  6.5 1186.6 %copy-start = (bf16[1,128,3584]{2,1,0:T(8,128)(2,1)S(1)}, bf16[1,128,3584]{2,1,0:T(8,128)(2,1)}, u32[]{:S(2)}) copy-start(bf16[1,128,3584]{2,1,0:T(8,128)(2,1)} %param.23) | copy-start | bytes 2752516
  6.5 72.8 %all-reduce.15.cloned.1.call-start = ((), (), s32[]{:S(2)}) async-start(), calls=%async_computation.8 | async-start | bytes 262144 | tf_op jit(solution)/shard_map/psum | solution.py:65
  8.0 2.8 copy-start.5
  13.2 17.6 copy-start.10
  80.4 34.4 %copy-start.4 = (bf16[2,32,3584]{2,1,0:T(8,128)(2,1)S(1)}, bf16[2,32,3584]{2,1,0:T(8,128)(2,1)}, u32[]{:S(2)}) copy-start(bf16[2,32,3584]{2,1,0:T(8,128)(2,1)} %param.17) | copy-start | bytes 1376260
  80.4 34.4 %copy-start.7 = (bf16[2,512,32]{1,2,0:T(8,128)(2,1)S(1)}, bf16[2,512,32]{1,2,0:T(8,128)(2,1)}, u32[]{:S(2)}) copy-start(bf16[2,512,32]{1,2,0:T(8,128)(2,1)} %param.16) | copy-start | bytes 196612
  82.6 18.8 all-to-all-start
  101.4 12.9 all-to-all-start.1
  106.1 1069.9 %all-reduce.13.cloned.1.call-start = ((), (), s32[]{:S(2)}) async-start(), calls=%async_computation.7 | async-start | bytes 1835008 | tf_op jit(solution)/shard_map/psum | solution.py:75
  116.0 1.3 copy-start.9
  116.0 1.6 copy-start.8
  116.0 1060.1 %copy-start.6 = (bf16[2,32,3584]{2,1,0:T(8,128)(2,1)S(1)}, bf16[2,32,3584]{2,1,0:T(8,128)(2,1)}, u32[]{:S(2)}) copy-start(bf16[2,32,3584]{2,1,0:T(8,128)(2,1)} %param.12) | copy-start | bytes 1376260
  117.2 1101.4 %reduce-scatter.3.cloned.1.call-start = ((), (), s32[]{:S(2)}) async-start(), calls=%async_computation.4 | async-start | bytes 573440 | tf_op jit(solution)/shard_map/reduce_scatter | solution.py:98
  1176.1 16.4 copy-start.1
  1177.5 15.2 copy-start.3
  1177.6 15.2 copy-start.2
  1194.2 55.6 %reduce-scatter.5.cloned.1.call-start = ((), (), s32[]{:S(2)}) async-start(), calls=%async_computation.5 | async-start | bytes 573440 | tf_op jit(solution)/shard_map/reduce_scatter | solution.py:98
  1207.8 1108.4 %all-reduce.11.cloned.1.call-start = ((), (), s32[]{:S(2)}) async-start(), calls=%async_computation.6 | async-start | bytes 1835008
Sparse Core Ops, SparseCore 0:
  24.9 54.4 all-reduce.14
  117.3 1058.7 all-reduce.12
  1194.3 24.1 reduce-scatter.2
  1221.5 28.2 reduce-scatter.4
  1252.6 1063.4 all-reduce.10
where the time goes:
time: 2330 us
  waiting for transfers between devices  2220 us (95%)
  blocking collectives  41.5 us (2%)
    unnamed x6, waiting for transfers between devices  1060 us
    psum x1, waiting for transfers between devices, body(): attended = lax.psum(partial_out, ('attn', 'exp'))  1060 us
    psum x1, waiting for transfers between devices, body(): lax.psum((local_acc * factor[:, None]).astype(jnp.bfloat16), 'attn')  48.5 us
  transfers between devices with their start and end apart: 7, of which 7 were waited for; matrix products, arithmetic and copies ran while one was open for 0% of the time, Pallas kernels for 0%

commit v1 on v0

v1 whole, which is shorter than its diff:
```python
import jax
import jax.numpy as jnp
from jax import lax
from jax.experimental import pallas as pl
from jax.experimental.pallas import tpu as pltpu
from jax.sharding import PartitionSpec as P

MESH = pl.DeviceIdType.MESH
F32 = jnp.float32
BF16 = jnp.bfloat16
SCALE = (128 + 64) ** -0.5
NT = (((1,), (1,)), ((), ()))


def remote(src, dst, send_sem, recv_sem, device):
    return pltpu.make_async_remote_copy(
        src_ref=src,
        dst_ref=dst,
        send_sem=send_sem,
        recv_sem=recv_sem,
        device_id=device,
        device_id_type=MESH,
    )


class Sends:
    def __init__(self, sems):
        self.sems = sems
        self.used = 0
        self.pending = []

    def go(self, src, dst, recv_sem, device, *conds):
        copy = remote(src, dst, self.sems.at[self.used], recv_sem, device)
        self.used += 1
        cond = None
        for item in conds:
            cond = item if cond is None else cond & item
        if cond is None:
            copy.start()
        else:
            pl.when(cond)(copy.start)
        self.pending.append((cond, copy))

    def drain(self):
        for cond, copy in self.pending:
            if cond is None:
                copy.wait_send()
            else:
                pl.when(cond)(copy.wait_send)
        self.pending = []


SEND_SEMS = 140


def kernel(
    len_ref,
    gain_ref,
    q_hbm,
    cache_hbm,
    resid_hbm,
    ids_hbm,
    wts_hbm,
    wv_hbm,
    wo_hbm,
    wg_hbm,
    wu_hbm,
    wd_hbm,
    out_ref,
    q_v,
    cache_v,
    res_v,
    ids_v,
    wts_v,
    wv_v,
    wvt_v,
    wo_v,
    wgu_v,
    wd_v,
    rw_v,
    s1_v,
    p1_v,
    c32_v,
    s2_v,
    p2_v,
    c2_v,
    s3_v,
    p3_v,
    hid_v,
    ag_v,
    pd_v,
    r0_v,
    qs_v,
    r1x_v,
    r1y_v,
    r1z_v,
    s1x_v,
    s1y_v,
    s1z_v,
    r2x_v,
    r2y_v,
    r2z_v,
    s2x_v,
    s2y_v,
    s2z_v,
    r3_v,
    f_v,
    o_v,
    lsem,
    send_sems,
    loop_sems,
    wsem,
    p1_sem,
    big_sem,
    g_sem,
    core_sem,
    r_sem,
):
    a = lax.axis_index("attn")
    g = lax.axis_index("grp")
    e = lax.axis_index("exp")
    c = e % 2
    y = (e // 2) % 8
    l = e // 16
    z = 2 * g + l
    yc = jnp.minimum(y, 6)
    has_tile = y < 7
    even = l == 0
    odd = l == 1
    first = c == 0
    second = c == 1
    sends = Sends(send_sems)
    when = pl.when

    def xi(d):
        return (a + d + 4) % 4

    def yi(d):
        return (y + d + 8) % 8

    def zi(d):
        return (z + d + 8) % 8

    def xdev(d):
        return {"attn": xi(d)}

    def ydev(d):
        return {"exp": l * 16 + yi(d) * 2 + c}

    def zdev(d):
        return {"grp": zi(d) // 2, "exp": (zi(d) % 2) * 16 + y * 2 + c}

    core_dev = {"exp": e + 1 - 2 * c}

    def arrived(dst, sem):
        remote(dst, dst, send_sems.at[0], sem, core_dev).wait_recv()

    chunk = pl.multiple_of((a * 7 + yc) * 128, 128)
    loads = [
        pltpu.make_async_copy(src, dst, lsem.at[i])
        for i, (src, dst) in enumerate(
            [
                (q_hbm, q_v),
                (cache_hbm, cache_v),
                (wv_hbm, wv_v),
                (
                    resid_hbm.at[l, pl.ds(pl.multiple_of(c * 16, 16), 16), pl.ds(chunk, 128)],
                    res_v,
                ),
                (ids_hbm, ids_v),
                (wts_hbm, wts_v),
                (
                    wo_hbm.at[:, :, pl.ds(pl.multiple_of(a * 896, 128), 896)],
                    wo_v.at[a],
                ),
                (wg_hbm, wgu_v.at[:, pl.ds(0, 128)]),
                (wu_hbm, wgu_v.at[:, pl.ds(128, 128)]),
                (wd_hbm, wd_v),
            ]
        )
    ]
    for load in loads:
        load.start()

    barrier = pltpu.get_barrier_semaphore()

    def greet(device):
        pl.semaphore_signal(barrier, inc=1, device_id=device, device_id_type=MESH)

    for d in range(1, 4):
        greet(xdev(d))
    for d in range(1, 8):
        greet(zdev(d))

    def greet_plane(i, carry):
        greet({"exp": (e + i) % 32})
        return carry

    lax.fori_loop(1, 32, greet_plane, 0)
    pl.semaphore_wait(barrier, 41)

    loads[0].wait()
    loads[1].wait()
    row = lax.broadcasted_iota(jnp.int32, (64, 64), 0)
    col = lax.broadcasted_iota(jnp.int32, (64, 64), 1)
    head = ((row & 15) >> 1) * 8 + (row >> 4) * 2 + (row & 1)
    perm = jnp.where(head == col, 1.0, 0.0).astype(BF16)
    pos = a * 512 + lax.broadcasted_iota(jnp.int32, (64, 512), 1)
    lane = lax.broadcasted_iota(jnp.int32, (64, 128), 1)
    for mb in range(2):
        qp = jnp.dot(perm, q_v[mb], preferred_element_type=F32).astype(BF16)
        scores = lax.dot_general(qp, cache_v[mb], NT, preferred_element_type=F32) * SCALE
        visible = pos < len_ref[mb, 0]
        top = jnp.max(jnp.where(visible, scores, -1e30), axis=1, keepdims=True)
        top = top.astype(BF16).astype(F32)
        weights = jnp.where(visible, jnp.exp(scores - top), 0.0)
        total = jnp.sum(weights, axis=1, keepdims=True)
        acc = jnp.dot(weights.astype(BF16), cache_v[mb, :, 0:512], preferred_element_type=F32)
        hi = total.astype(BF16).astype(F32)
        stats = jnp.where(lane == 0, top, jnp.where(lane == 1, hi, total - hi))
        s1_v[:, mb, :, 0:512] = acc.astype(BF16).reshape(4, 16, 512)
        s1_v[:, mb, :, 512:640] = stats.astype(BF16).reshape(4, 16, 128)
    for d in range(1, 4):
        sends.go(s1_v.at[xi(d)], p1_v.at[d - 1], p1_sem.at[d - 1], xdev(d))

    loads[2].wait()
    eye = jnp.where(
        lax.broadcasted_iota(jnp.int32, (32, 32), 0)
        == lax.broadcasted_iota(jnp.int32, (32, 32), 1),
        1.0,
        0.0,
    ).astype(BF16)
    for h in range(2):
        wvt_v[a, h] = lax.dot_general(eye, wv_v[h], NT, preferred_element_type=F32).astype(BF16)
    for d in range(1, 4):
        sends.go(wvt_v.at[a], wvt_v.at[a], wsem.at[d - 1], xdev(d))
        sends.go(
            wo_hbm.at[:, :, pl.ds(pl.multiple_of(xi(d) * 896, 128), 896)],
            wo_v.at[a],
            wsem.at[2 + d],
            xdev(d),
        )

    loads[4].wait()
    loads[5].wait()
    for mb in range(2):
        gate = jnp.sum(
            jnp.where(ids_v[mb] == e, wts_v[mb], 0.0), axis=1, keepdims=True
        )
        gate = jnp.broadcast_to(gate, (128, 128))
        for grp in range(4):
            at = (grp * 2 + mb) * 32
            rw_v[at : at + 32, :] = gate[grp * 32 : (grp + 1) * 32, :]

    for d in range(1, 4):
        arrived(p1_v.at[d - 1], p1_sem.at[d - 1])
    blocks = [s1_v[a]] + [p1_v[d] for d in range(3)]
    blocks = [b.astype(F32).reshape(32, 640) for b in blocks]
    tops = [b[:, 512:513] for b in blocks]
    row_top = jnp.maximum(jnp.maximum(tops[0], tops[1]), jnp.maximum(tops[2], tops[3]))
    ctx_sum = jnp.zeros((32, 512), F32)
    row_total = jnp.zeros((32, 1), F32)
    for b, t in zip(blocks, tops):
        factor = jnp.exp(t - row_top)
        ctx_sum = ctx_sum + b[:, 0:512] * factor
        row_total = row_total + (b[:, 513:514] + b[:, 514:515]) * factor
    context = ctx_sum / row_total
    for mb in range(2):
        for k in range(4):
            c32_v[:, mb * 4 + k, :] = context[
                mb * 16 : (mb + 1) * 16, k * 128 : (k + 1) * 128
            ]
    s2_v[...] = c32_v[...].reshape(8, 16, 128).astype(BF16)

    def p2_copy(i):
        j = (i // 4 + e) % 8
        to_a = (a + i) % 4
        to_e = 4 * j + a
        mine = (to_a == a) & (to_e == e)
        far = remote(
            s2_v.at[j],
            p2_v.at[e],
            loop_sems.at[i],
            big_sem.at[0],
            {"attn": to_a, "exp": to_e},
        )
        near = pltpu.make_async_copy(s2_v.at[j], p2_v.at[e], big_sem.at[0])
        return mine, far, near

    def p2_go(i, carry):
        mine, far, near = p2_copy(i)
        pl.when(mine)(near.start)
        pl.when(jnp.logical_not(mine))(far.start)
        return carry

    def p2_done(i, carry):
        mine, far, near = p2_copy(i)
        pl.when(jnp.logical_not(mine))(far.wait_send)
        return carry

    lax.fori_loop(0, 32, p2_go, 0)

    loads[6].wait()
    for d in range(1, 4):
        arrived(wvt_v.at[xi(-d)], wsem.at[d - 1])
        arrived(wo_v.at[xi(-d)], wsem.at[2 + d])
    pltpu.make_async_copy(p2_v, p2_v, big_sem.at[0]).wait()
    c2_v[...] = p2_v[...].astype(F32)
    out = jnp.zeros((64, 896), F32)
    for h in range(2):
        rows = [
            jnp.concatenate([c2_v[:, h * 8 + mb * 4 + k, :] for k in range(4)], axis=1)
            for mb in range(2)
        ]
        ctx = jnp.concatenate(rows, axis=0).astype(BF16)
        values = lax.dot_general(
            ctx, wvt_v[:, h].reshape(128, 512), NT, preferred_element_type=F32
        ).astype(BF16)
        out = out + jnp.dot(
            values, wo_v[:, h].reshape(128, 896), preferred_element_type=F32
        )
    for k in range(7):
        s3_v[k] = out[:, k * 128 : (k + 1) * 128].astype(BF16).reshape(4, 16, 128)

    def p3_copy(i):
        to_e = (e + i) % 32
        to_y = (to_e // 2) % 8
        tile = (to_e // 16) * 2 + to_e % 2
        src = s3_v.at[jnp.minimum(to_y, 6), tile]
        far = remote(src, p3_v.at[e], loop_sems.at[32 + i], big_sem.at[1], {"exp": to_e})
        return to_y < 7, far

    def p3_go(i, carry):
        used, far = p3_copy(i)
        pl.when(used)(far.start)
        return carry

    def p3_done(i, carry):
        used, far = p3_copy(i)
        pl.when(used)(far.wait_send)
        return carry

    lax.fori_loop(1, 32, p3_go, 0)

    @when(has_tile)
    def _():
        pltpu.make_async_copy(s3_v.at[yc, l * 2 + c], p3_v.at[e], big_sem.at[1]).start()
        loads[3].wait()
        pltpu.make_async_copy(p3_v, p3_v, big_sem.at[1]).wait()
        attended = jnp.sum(p3_v[...].astype(F32), axis=0)
        hidden = res_v[...].astype(F32) + attended
        hid_v[...] = hidden
        ag_v[a, yc, g, l, c] = (hidden * gain_ref[pl.ds(a * 7 + yc, 1), :]).astype(BF16)

    @when(jnp.logical_not(has_tile))
    def _():
        loads[3].wait()

    own = ag_v.at[a, yc, g, l, c]
    for d in range(1, 8):
        sends.go(own, own, g_sem.at[d - 1], ydev(d), even, has_tile)
    for d in range(1, 8):
        sends.go(own, own, g_sem.at[7 + d - 1], zdev(d), odd, first, has_tile)
    for d in range(1, 4):
        sends.go(own, own, g_sem.at[14 + d - 1], xdev(d), odd, second, has_tile)

    @when(even)
    def _():
        for d in range(1, 8):

            @when(yi(-d) < 7)
            def _():
                arrived(ag_v.at[a, jnp.minimum(yi(-d), 6), g, 0, c], g_sem.at[d - 1])

    for d in range(1, 8):
        blk = ag_v.at[a, :, g, 0, c]
        sends.go(blk, blk, g_sem.at[17 + d - 1], zdev(d), even)

    @when(first & has_tile)
    def _():
        for d in range(1, 8):

            @when(zi(-d) % 2 == 1)
            def _():
                arrived(ag_v.at[a, yc, zi(-d) // 2, 1, 0], g_sem.at[7 + d - 1])

    for d in range(1, 4):
        blk = ag_v.at[a, yc, :, 1, 0]
        sends.go(blk, blk, g_sem.at[24 + d - 1], xdev(d), first, has_tile)

    @when(odd & second & has_tile)
    def _():
        for d in range(1, 4):
            arrived(ag_v.at[xi(-d), yc, g, 1, 1], g_sem.at[14 + d - 1])

    for d in range(1, 8):
        blk = ag_v.at[:, yc, g, 1, 1]
        sends.go(blk, blk, g_sem.at[27 + d - 1], ydev(d), odd, second, has_tile)

    for d in range(1, 8):

        @when(zi(-d) % 2 == 0)
        def _():
            arrived(ag_v.at[a, :, zi(-d) // 2, 0, c], g_sem.at[17 + d - 1])

    blk_x = ag_v.at[a, :, :, 0, c]
    for d in range(1, 4):
        sends.go(blk_x, blk_x, g_sem.at[34 + d - 1], xdev(d))
    sends.go(blk_x, blk_x, core_sem.at[0], core_dev)

    @when(first & has_tile)
    def _():
        for d in range(1, 4):
            arrived(ag_v.at[xi(-d), yc, :, 1, 0], g_sem.at[24 + d - 1])

    blk_y = ag_v.at[:, yc, :, 1, 0]
    for d in range(1, 8):
        sends.go(blk_y, blk_y, g_sem.at[37 + d - 1], ydev(d), first, has_tile)
    sends.go(blk_y, blk_y, core_sem.at[4], core_dev, first, has_tile)

    @when(odd & second)
    def _():
        for d in range(1, 8):

            @when(yi(-d) < 7)
            def _():
                arrived(ag_v.at[:, jnp.minimum(yi(-d), 6), g, 1, 1], g_sem.at[27 + d - 1])

    blk_z = ag_v.at[:, :, g, 1, 1]
    for d in range(1, 8):
        sends.go(blk_z, blk_z, g_sem.at[44 + d - 1], zdev(d), odd, second)
    sends.go(blk_z, blk_z, core_sem.at[12], core_dev, odd, second)

    for d in range(1, 4):
        blk = ag_v.at[xi(-d), :, :, 0, c]
        arrived(blk, g_sem.at[34 + d - 1])
        sends.go(blk, blk, core_sem.at[d], core_dev)
    for d in range(1, 8):
        cond = first & (yi(-d) < 7)
        blk = ag_v.at[:, jnp.minimum(yi(-d), 6), :, 1, 0]

        @when(cond)
        def _():
            arrived(blk, g_sem.at[37 + d - 1])

        sends.go(blk, blk, core_sem.at[4 + d], core_dev, cond)
    for d in range(1, 8):
        cond = second & (zi(-d) % 2 == 1)
        blk = ag_v.at[:, :, zi(-d) // 2, 1, 1]

        @when(cond)
        def _():
            arrived(blk, g_sem.at[44 + d - 1])

        sends.go(blk, blk, core_sem.at[12 + d], core_dev, cond)
    for d in range(4):
        arrived(ag_v.at[xi(-d), :, :, 0, 1 - c], core_sem.at[d])
    for d in range(8):

        @when(second & (yi(-d) < 7))
        def _():
            arrived(ag_v.at[:, jnp.minimum(yi(-d), 6), :, 1, 0], core_sem.at[4 + d])

        @when(first & (zi(-d) % 2 == 1))
        def _():
            arrived(ag_v.at[:, :, zi(-d) // 2, 1, 1], core_sem.at[12 + d])

    loads[7].wait()
    loads[8].wait()
    loads[9].wait()
    pieces = [ag_v[i // 7, i % 7].reshape(256, 128) for i in range(28)]
    square = jnp.zeros((256, 128), F32)
    for i in range(28):
        item = pieces[i].astype(F32) / gain_ref[i : i + 1, :]
        square = square + item * item
    inverse = lax.rsqrt(jnp.sum(square, axis=1, keepdims=True) * (1.0 / 3584) + 1e-6)
    both = jnp.dot(jnp.concatenate(pieces, axis=1), wgu_v[...], preferred_element_type=F32)
    both = both * inverse
    gate = both[:, 0:128]
    act = gate / (1.0 + jnp.exp(-gate)) * both[:, 128:256] * rw_v[...]
    act = act.astype(BF16)
    for d in (1, 2, 3, 0):
        x = xi(d)
        down = jnp.dot(
            act,
            wd_v[:, pl.ds(pl.multiple_of(x * 896, 128), 896)],
            preferred_element_type=F32,
        )
        for k in range(7):
            pd_v[x, k] = (
                down[:, k * 128 : (k + 1) * 128].astype(BF16).reshape(4, 2, 2, 16, 128)
            )
        sends.go(pd_v.at[x, :, :, :, 1 - c], r0_v.at[x], r_sem.at[d], core_dev)

    for d in (1, 2, 3, 0):
        x = xi(d)
        arrived(r0_v.at[x], r_sem.at[d])
        qs_v[x] = (pd_v[x, :, :, :, c].astype(F32) + r0_v[x].astype(F32)).astype(BF16)
        if d > 0:
            sends.go(qs_v.at[x, :, :, 0], r1x_v.at[d - 1], r_sem.at[4 + d - 1], xdev(d))
    for d in range(1, 8):
        sends.go(
            qs_v.at[:, jnp.minimum(yi(d), 6), :, 1],
            r1y_v.at[d - 1],
            r_sem.at[7 + d - 1],
            ydev(d),
            first,
            yi(d) < 7,
        )
    for d in range(1, 8):
        sends.go(
            qs_v.at[:, :, zi(d) // 2, 1],
            r1z_v.at[d - 1],
            r_sem.at[14 + d - 1],
            zdev(d),
            second,
            zi(d) % 2 == 1,
        )

    def total_of(own_block, ref, count):
        result = own_block.astype(F32)
        for i in range(count):
            result = result + ref[i].astype(F32)
        return result

    def all_arrived(ref, base, count):
        for i in range(count):
            arrived(ref.at[i], r_sem.at[base + i])

    all_arrived(r1x_v, 4, 3)
    s1x_v[...] = total_of(qs_v[a, :, :, 0], r1x_v, 3).astype(BF16)
    for d in range(1, 8):
        sends.go(
            s1x_v.at[:, zi(d) // 2],
            r2x_v.at[d - 1],
            r_sem.at[21 + d - 1],
            zdev(d),
            zi(d) % 2 == 0,
        )

    @when(first & has_tile)
    def _():
        all_arrived(r1y_v, 7, 7)
        s1y_v[...] = total_of(qs_v[:, yc, :, 1], r1y_v, 7).astype(BF16)

    for d in range(1, 4):
        sends.go(
            s1y_v.at[xi(d)],
            r2y_v.at[d - 1],
            r_sem.at[28 + d - 1],
            xdev(d),
            first,
            has_tile,
        )

    @when(second & odd)
    def _():
        all_arrived(r1z_v, 14, 7)
        s1z_v[...] = total_of(qs_v[:, :, g, 1], r1z_v, 7).astype(BF16)

    for d in range(1, 8):
        sends.go(
            s1z_v.at[:, jnp.minimum(yi(d), 6)],
            r2z_v.at[d - 1],
            r_sem.at[31 + d - 1],
            ydev(d),
            second,
            odd,
            yi(d) < 7,
        )

    @when(even)
    def _():
        all_arrived(r2x_v, 21, 7)
        s2x_v[...] = total_of(s1x_v[:, g], r2x_v, 7).astype(BF16)

    for d in range(1, 8):
        sends.go(
            s2x_v.at[jnp.minimum(yi(d), 6)],
            r3_v.at[d - 1],
            r_sem.at[38 + d - 1],
            ydev(d),
            even,
            yi(d) < 7,
        )

    @when(first & has_tile)
    def _():
        all_arrived(r2y_v, 28, 3)
        s2y_v[...] = total_of(s1y_v[a], r2y_v, 3).astype(BF16)

    for d in range(1, 8):
        sends.go(
            s2y_v.at[zi(d) // 2],
            r3_v.at[d - 1],
            r_sem.at[38 + d - 1],
            zdev(d),
            first,
            has_tile,
            zi(d) % 2 == 1,
        )

    @when(second & odd & has_tile)
    def _():
        all_arrived(r2z_v, 31, 7)
        s2z_v[...] = total_of(s1z_v[:, yc], r2z_v, 7).astype(BF16)

    for d in range(1, 4):
        sends.go(
            s2z_v.at[xi(d)],
            r3_v.at[d - 1],
            r_sem.at[38 + d - 1],
            xdev(d),
            second,
            odd,
            has_tile,
        )

    def put_rows(tile):
        for i in range(16):
            f_v[i] = tile[i : i + 1, :]

    @when(even & has_tile)
    def _():
        all_arrived(r3_v, 38, 7)
        put_rows(hid_v[...] + total_of(s2x_v[yc], r3_v, 7))

    @when(odd & first & has_tile)
    def _():
        all_arrived(r3_v, 38, 7)
        put_rows(hid_v[...] + total_of(s2y_v[g], r3_v, 7))

    @when(odd & second & has_tile)
    def _():
        all_arrived(r3_v, 38, 3)
        put_rows(hid_v[...] + total_of(s2z_v[a], r3_v, 3))

    def last_copy(i):
        to_e = c * 16 + i
        far = remote(
            f_v.at[i], o_v.at[l, yc], loop_sems.at[64 + i], big_sem.at[2], {"exp": to_e}
        )
        near = pltpu.make_async_copy(f_v.at[i], o_v.at[l, yc], big_sem.at[2])
        return to_e == e, far, near

    def last_go(i, carry):
        mine, far, near = last_copy(i)
        pl.when(mine)(near.start)
        pl.when(jnp.logical_not(mine))(far.start)
        return carry

    def last_done(i, carry):
        mine, far, near = last_copy(i)
        pl.when(jnp.logical_not(mine))(far.wait_send)
        return carry

    @when(has_tile)
    def _():
        lax.fori_loop(0, 16, last_go, 0)

    lax.fori_loop(0, 32, p2_done, 0)
    lax.fori_loop(1, 32, p3_done, 0)
    sends.drain()

    @when(has_tile)
    def _():
        lax.fori_loop(0, 16, last_done, 0)

    pltpu.make_async_copy(o_v, o_v, big_sem.at[2]).wait()
    for mb in range(2):
        out_ref[mb] = jnp.concatenate([o_v[mb, k] for k in range(7)], axis=1).astype(BF16)


def body(
    resid,
    queries,
    cache,
    lengths,
    w_value,
    w_out,
    norm_gain,
    route_ids,
    route_weights,
    w_gate,
    w_up,
    w_down,
):
    hbm = pl.BlockSpec(memory_space=pl.ANY)
    vmem = pl.BlockSpec(memory_space=pltpu.VMEM)
    smem = pl.BlockSpec(memory_space=pltpu.SMEM)

    def bf(*shape):
        return pltpu.VMEM(shape, BF16)

    def f32(*shape):
        return pltpu.VMEM(shape, F32)

    def dma(count):
        return pltpu.SemaphoreType.DMA((count,))

    return pl.pallas_call(
        kernel,
        out_shape=jax.ShapeDtypeStruct((2, 1, 896), BF16),
        in_specs=[smem, vmem] + [hbm] * 10,
        out_specs=vmem,
        scratch_shapes=[
            bf(2, 64, 576),
            bf(2, 512, 576),
            bf(16, 128),
            pltpu.VMEM((2, 128, 8), jnp.int32),
            f32(2, 128, 8),
            bf(2, 512, 32),
            bf(4, 2, 32, 512),
            bf(4, 2, 32, 896),
            bf(3584, 256),
            bf(128, 3584),
            f32(256, 128),
            bf(4, 2, 16, 640),
            bf(3, 2, 16, 640),
            f32(16, 8, 128),
            bf(8, 16, 128),
            bf(32, 16, 128),
            f32(32, 16, 128),
            bf(7, 4, 16, 128),
            bf(32, 16, 128),
            f32(16, 128),
            bf(4, 7, 4, 2, 2, 16, 128),
            bf(4, 7, 4, 2, 2, 16, 128),
            bf(4, 7, 4, 2, 16, 128),
            bf(4, 7, 4, 2, 16, 128),
            bf(3, 7, 4, 16, 128),
            bf(7, 4, 4, 16, 128),
            bf(7, 4, 7, 16, 128),
            bf(7, 4, 16, 128),
            bf(4, 4, 16, 128),
            bf(4, 7, 16, 128),
            bf(7, 7, 16, 128),
            bf(3, 4, 16, 128),
            bf(7, 4, 16, 128),
            bf(7, 16, 128),
            bf(4, 16, 128),
            bf(4, 16, 128),
            bf(7, 16, 128),
            f32(16, 1, 128),
            f32(2, 7, 1, 128),
            dma(10),
            dma(SEND_SEMS),
            dma(80),
            dma(6),
            dma(3),
            dma(3),
            dma(51),
            dma(20),
            dma(45),
        ],
        compiler_params=pltpu.CompilerParams(
            collective_id=0, has_side_effects=True, vmem_limit_bytes=56 * 1024 * 1024
        ),
        name="layer",
    )(
        lengths,
        norm_gain.astype(F32).reshape(28, 128),
        queries[:, 0],
        cache[:, 0],
        resid,
        route_ids,
        route_weights,
        w_value,
        w_out,
        w_gate[0],
        w_up[0],
        w_down[0],
    )


def solution(mesh):
    return jax.shard_map(
        body,
        mesh=mesh,
        in_specs=(
            P(None, "grp", None),
            P(None, ("grp", "exp"), None, None),
            P(None, ("grp", "exp"), "attn", None),
            P(None, ("grp", "exp")),
            P("exp", None, "attn"),
            P("exp", "attn", None),
            P(),
            P(),
            P(),
            P("exp", None, ("attn", "grp")),
            P("exp", None, ("attn", "grp")),
            P("exp", ("attn", "grp"), None),
        ),
        out_specs=P(None, ("grp", "exp"), "attn"),
        check_vma=False,
    )
```

time: 2330 us -> 102 us (0.04)
  waiting for transfers between devices: 2220 us -> 0 us
  Pallas kernels: 0 us -> 90.2 us
  blocking collectives: 41.5 us -> 0 us
    psum x2 -> x0, waiting for transfers between devices: 1110 us -> none  [the longest x1 1060 us: body(): attended = lax.psum(partial_out, ('attn', 'exp'))]
    unnamed x6 -> x0, waiting for transfers between devices: 1060 us -> none
    pallas_call x0 -> x1, Pallas kernels: none -> 90.2 us  [body(): pl.pallas_call(kernel, out_shape=jax.ShapeDtypeStruct((2, 1, 896), BF16),...]
    reduce_scatter x2 -> x0, waiting for transfers between devices: 39.7 us -> none  [body(): lax.psum_scatter(partial_down.reshape(grp_count, capacity, model_width).a...]
    all_gather x2 -> x0, blocking collectives: 26.2 us -> none  [body(): piece_rows = lax.all_gather(picked, 'grp', axis=0, tiled=True)]
  transfers between devices with their start and end apart: 7 -> 0, of which waited for: 7 -> 0; matrix products, arithmetic and copies ran while one was open for 0% -> 0% of each run, Pallas kernels for 0% -> 0%
where the time goes in v1:
time: 102 us; the launch traced here: 101 us
  Pallas kernels  90.2 us (88%)
  local copies, waits for them, and re-layouts  9.63 us (9%)
  other arithmetic  1.3 us (1%)
    pallas_call x1, Pallas kernels, body(): pl.pallas_call(kernel, out_shape=jax.ShapeDtypeStruct((2, 1, 896), BF16),...  90.2 us
    unnamed x5, local copies, waits for them, and re-layouts  8.36 us

profile of v1, /device:TPU:1, one launch (start us, length us, event | category | flops | bytes accessed | tf_op | source)
XLA Modules:
  0.0 101.1 jit_solution(3650547464874342750)
XLA Ops:
  0.0 1.3 %copy.14.len_ref = s32[2,1]{1,0:T(2,128)} copy(s32[2,1]{0,1:T(1,128)} %param.15) | data formatting | bytes 16 | tf_op args[3]
  1.3 1.3 %bitcast_convert_fusion.gain_ref = f32[28,128]{1,0:T(8,128)} fusion(bf16[3584]{0:T(1024)(128)(2,1)} %param.18), kind=kLoop, calls=%fused_computation | loop fusion | flops 3584 | bytes 21504 | tf_op jit(solution)/shard_map/reshape | solution.py:762
  2.6 1.5 %copy.15.ids_hbm = s32[2,128,8]{2,1,0:T(8,128)} copy(s32[2,128,8]{1,2,0:T(8,128)} %param.19) | data formatting | bytes 16384 | tf_op args[7]
  4.1 1.5 %copy.16.wts_hbm = f32[2,128,8]{2,1,0:T(8,128)} copy(f32[2,128,8]{1,2,0:T(8,128)} %param.20) | data formatting | bytes 16384 | tf_op args[8]
  5.5 1.7 %copy.17.wv_hbm = bf16[2,512,32]{2,1,0:T(8,128)(2,1)} copy(bf16[2,512,32]{1,2,0:T(8,128)(2,1)} %param.16) | data formatting | bytes 131072 | tf_op args[4]
  7.2 2.4 %copy.13 = bf16[2,1,512,576]{3,2,0,1:T(8,128)(2,1)} copy(bf16[2,1,512,576]{2,3,1,0:T(8,128)(2,1)} %param.14) | data formatting | bytes 2359296 | tf_op args[2]
  9.7 90.2 %layer.1 = bf16[2,1,896]{2,1,0:T(2,128)(2,1)} custom-call(s32[2,1]{1,0:T(2,128)} %copy.14.len_ref, f32[28,128]{1,0:T(8,128)} %bitcast_convert_fusion.gain_ref, bf16[2,64,576]{2,1,0:T(8,128)(2,1)} %bitcast.12, bf16[2,512,576]{2,1,0:T(8,128)(2,1)} %bitcast.8, bf16[2,32,3584]{2,1,0:T(8,128)(2,1)} %resid_hbm.1, s32[2,128,8]{2,1,0:T(8,128)} %copy.15.ids_hbm, ...), custom_call_target="tpu_custom_call" | custom-call | tf_op jit(solution)/shard_map/layer/pallas_call | solution.py:701
  99.8 1.3 %copy.18 = bf16[2,1,896]{2,0,1:T(2,128)(2,1)} copy(bf16[2,1,896]{2,1,0:T(2,128)(2,1)} %layer.1) | data formatting | bytes 7168 | tf_op jit(solution)/shard_map/layer/pallas_call | solution.py:701

commit v2 on v1

v2 whole, which is shorter than its diff:
```python
import jax
import jax.numpy as jnp
from jax import lax
from jax.experimental import pallas as pl
from jax.experimental.pallas import tpu as pltpu
from jax.sharding import PartitionSpec as P

MESH = pl.DeviceIdType.MESH
F32 = jnp.float32
BF16 = jnp.bfloat16
SCALE = (128 + 64) ** -0.5
NT = (((1,), (1,)), ((), ()))


def remote(src, dst, send_sem, recv_sem, device):
    return pltpu.make_async_remote_copy(
        src_ref=src,
        dst_ref=dst,
        send_sem=send_sem,
        recv_sem=recv_sem,
        device_id=device,
        device_id_type=MESH,
    )


class Sends:
    def __init__(self, sems):
        self.sems = sems
        self.used = 0
        self.pending = []

    def go(self, src, dst, recv_sem, device, *conds):
        copy = remote(src, dst, self.sems.at[self.used], recv_sem, device)
        self.used += 1
        cond = None
        for item in conds:
            cond = item if cond is None else cond & item
        if cond is None:
            copy.start()
        else:
            pl.when(cond)(copy.start)
        self.pending.append((cond, copy))

    def drain(self):
        for cond, copy in self.pending:
            if cond is None:
                copy.wait_send()
            else:
                pl.when(cond)(copy.wait_send)
        self.pending = []


FAR8 = (4, 3, 5, 2, 6, 1, 7)
FAR4 = (2, 1, 3)
NEAR8 = (1, 7, 2, 6, 3, 5, 4)
NEAR4 = (1, 3, 2)
SEND_SEMS = 232


def kernel(
    len_ref,
    gain_ref,
    q_hbm,
    cache_hbm,
    resid_hbm,
    ids_hbm,
    wts_hbm,
    wv_hbm,
    wo_hbm,
    wg_hbm,
    wu_hbm,
    wd_hbm,
    out_ref,
    q_v,
    cache_v,
    res_v,
    ids_v,
    wts_v,
    wvt_v,
    wo_v,
    wgu_v,
    wd_v,
    rw_v,
    gain_v,
    s1_v,
    p1_v,
    c32_v,
    s2_v,
    p2_v,
    c2_v,
    s3_v,
    p3_v,
    hid_v,
    ag_v,
    pd_v,
    r0_v,
    qs_v,
    r1x_v,
    r1y_v,
    r1z_v,
    s1x_v,
    s1y_v,
    s1z_v,
    r2x_v,
    r2y_v,
    r2z_v,
    s2x_v,
    s2y_v,
    s2z_v,
    r3_v,
    f_v,
    o_v,
    unit_v,
    fin_v,
    lsem,
    send_sems,
    loop_sems,
    wsem,
    p1_sem,
    big_sem,
    g_sem,
    core_sem,
    r_sem,
):
    a = lax.axis_index("attn")
    g = lax.axis_index("grp")
    e = lax.axis_index("exp")
    c = e % 2
    y = (e // 2) % 8
    l = e // 16
    z = 2 * g + l
    yc = jnp.minimum(y, 6)
    has_tile = y < 7
    even = l == 0
    odd = l == 1
    first = c == 0
    second = c == 1
    sends = Sends(send_sems)
    when = pl.when

    def xi(d):
        return (a + d + 4) % 4

    def yi(d):
        return (y + d + 8) % 8

    def zi(d):
        return (z + d + 8) % 8

    def xdev(d):
        return {"attn": xi(d)}

    def ydev(d):
        return {"exp": l * 16 + yi(d) * 2 + c}

    def zdev(d):
        return {"grp": zi(d) // 2, "exp": (zi(d) % 2) * 16 + y * 2 + c}

    core_dev = {"exp": e + 1 - 2 * c}

    def arrived(dst, sem):
        remote(dst, dst, send_sems.at[0], sem, core_dev).wait_recv()

    chunk = pl.multiple_of((a * 7 + yc) * 128, 128)
    loads = [
        pltpu.make_async_copy(src, dst, lsem.at[i])
        for i, (src, dst) in enumerate(
            [
                (q_hbm, q_v),
                (cache_hbm, cache_v),
                (wv_hbm, wvt_v.at[a]),
                (
                    resid_hbm.at[l, pl.ds(pl.multiple_of(c * 16, 16), 16), pl.ds(chunk, 128)],
                    res_v,
                ),
                (ids_hbm, ids_v),
                (wts_hbm, wts_v),
                (
                    wo_hbm.at[:, :, pl.ds(pl.multiple_of(a * 896, 128), 896)],
                    wo_v.at[a],
                ),
                (wg_hbm, wgu_v.at[:, pl.ds(0, 128)]),
                (wu_hbm, wgu_v.at[:, pl.ds(128, 128)]),
                (wd_hbm, wd_v),
            ]
        )
    ]
    for load in loads:
        load.start()

    barrier = pltpu.get_barrier_semaphore()

    def greet(device):
        pl.semaphore_signal(barrier, inc=1, device_id=device, device_id_type=MESH)


    def greet_plane(i, carry):
        greet({"exp": (e + i) % 32})
        return carry

    lax.fori_loop(8, 32, greet_plane, 0)
    for d in FAR8:
        greet(zdev(d))
    for d in FAR4:
        greet(xdev(d))
    lax.fori_loop(1, 8, greet_plane, 0)

    gain_v[...] = gain_ref[...].astype(F32)
    unit_v[:, :, 8:16, :] = jnp.zeros((2, 128, 8, 128), F32)

    loads[0].wait()
    loads[1].wait()
    row = lax.broadcasted_iota(jnp.int32, (64, 64), 0)
    col = lax.broadcasted_iota(jnp.int32, (64, 64), 1)
    head = ((row & 15) >> 1) * 8 + (row >> 4) * 2 + (row & 1)
    perm = jnp.where(head == col, 1.0, 0.0).astype(BF16)
    pos = a * 512 + lax.broadcasted_iota(jnp.int32, (64, 512), 1)
    lane = lax.broadcasted_iota(jnp.int32, (64, 128), 1)
    for mb in range(2):
        qp = jnp.dot(perm, q_v[mb], preferred_element_type=F32).astype(BF16)
        scores = jnp.dot(qp, cache_v[mb], preferred_element_type=F32) * SCALE
        visible = pos < len_ref[0, mb]
        top = jnp.max(jnp.where(visible, scores, -1e30), axis=1, keepdims=True)
        top = top.astype(BF16).astype(F32)
        weights = jnp.where(visible, jnp.exp(scores - top), 0.0)
        total = jnp.sum(weights, axis=1, keepdims=True)
        acc = lax.dot_general(
            weights.astype(BF16), cache_v[mb, 0:512, :], NT, preferred_element_type=F32
        )
        hi = total.astype(BF16).astype(F32)
        stats = jnp.where(lane == 0, top, jnp.where(lane == 1, hi, total - hi))
        s1_v[:, mb, :, 0:512] = acc.astype(BF16).reshape(4, 16, 512)
        s1_v[:, mb, :, 512:640] = stats.astype(BF16).reshape(4, 16, 128)
    pl.semaphore_wait(barrier, 41)
    for d in FAR4:
        sends.go(s1_v.at[xi(d)], p1_v.at[d - 1], p1_sem.at[d - 1], xdev(d))

    loads[4].wait()
    loads[5].wait()
    for mb in range(2):
        gate = jnp.sum(
            jnp.where(ids_v[mb] == e, wts_v[mb], 0.0), axis=0, keepdims=True
        )
        gate = jnp.broadcast_to(gate, (128, 128)).T
        for grp in range(4):
            at = (grp * 2 + mb) * 32
            rw_v[at : at + 32, :] = gate[grp * 32 : (grp + 1) * 32, :]

    loads[2].wait()
    for d in FAR4:
        sends.go(wvt_v.at[a], wvt_v.at[a], wsem.at[d - 1], xdev(d))

    for d in range(1, 4):
        arrived(p1_v.at[d - 1], p1_sem.at[d - 1])
    blocks = [s1_v[a]] + [p1_v[d] for d in range(3)]
    blocks = [b.astype(F32).reshape(32, 640) for b in blocks]
    tops = [b[:, 512:513] for b in blocks]
    row_top = jnp.maximum(jnp.maximum(tops[0], tops[1]), jnp.maximum(tops[2], tops[3]))
    ctx_sum = jnp.zeros((32, 512), F32)
    row_total = jnp.zeros((32, 1), F32)
    for b, t in zip(blocks, tops):
        factor = jnp.exp(t - row_top)
        ctx_sum = ctx_sum + b[:, 0:512] * factor
        row_total = row_total + (b[:, 513:514] + b[:, 514:515]) * factor
    context = ctx_sum / row_total
    for mb in range(2):
        for k in range(4):
            c32_v[:, mb * 4 + k, :] = context[
                mb * 16 : (mb + 1) * 16, k * 128 : (k + 1) * 128
            ]
    s2_v[...] = c32_v[...].reshape(8, 16, 128).astype(BF16)

    for s_off in (2, 1, 3, 0):
        for d in FAR4 + (0,):
            for half in (1, 0):
                j = (half + l) % 2 * 4 + (y // 2 + s_off) % 4
                to_e = 4 * j + a
                device = {"attn": xi(d), "exp": to_e}
                if s_off == 0 and d == 0:
                    mine = to_e == e
                    near = pltpu.make_async_copy(s2_v.at[j], p2_v.at[e], big_sem.at[0])
                    when(mine)(near.start)
                    sends.go(
                        s2_v.at[j], p2_v.at[e], big_sem.at[0], device, jnp.logical_not(mine)
                    )
                else:
                    sends.go(s2_v.at[j], p2_v.at[e], big_sem.at[0], device)

    for d in FAR4:
        sends.go(
            wo_hbm.at[:, :, pl.ds(pl.multiple_of(xi(d) * 896, 128), 896)],
            wo_v.at[a],
            wsem.at[2 + d],
            xdev(d),
        )
    loads[6].wait()
    for d in range(1, 4):
        arrived(wvt_v.at[xi(-d)], wsem.at[d - 1])
        arrived(wo_v.at[xi(-d)], wsem.at[2 + d])
    pltpu.make_async_copy(p2_v, p2_v, big_sem.at[0]).wait()
    c2_v[...] = p2_v[...].astype(F32)
    out = jnp.zeros((64, 896), F32)
    for h in range(2):
        rows = [
            jnp.concatenate([c2_v[:, h * 8 + mb * 4 + k, :] for k in range(4)], axis=1)
            for mb in range(2)
        ]
        ctx = jnp.concatenate(rows, axis=0).astype(BF16)
        values = lax.dot_general(
            ctx, wvt_v[:, h].reshape(128, 512), NT, preferred_element_type=F32
        ).astype(BF16)
        out = out + jnp.dot(
            values, wo_v[:, h].reshape(128, 896), preferred_element_type=F32
        )
    for k in range(7):
        s3_v[k] = out[:, k * 128 : (k + 1) * 128].astype(BF16).reshape(4, 16, 128)

    for d in FAR8 + (0,):
        for half in (1, 0):
            for core in (1, 0):
                if d == 0 and half == 0 and core == 0:
                    continue
                to_l, to_c = (l + half) % 2, (c + core) % 2
                src = s3_v.at[jnp.minimum(yi(d), 6), to_l * 2 + to_c]
                device = {"exp": to_l * 16 + yi(d) * 2 + to_c}
                sends.go(src, p3_v.at[e], big_sem.at[1], device, yi(d) < 7)

    @when(has_tile)
    def _():
        pltpu.make_async_copy(s3_v.at[yc, l * 2 + c], p3_v.at[e], big_sem.at[1]).start()
        loads[3].wait()
        pltpu.make_async_copy(p3_v, p3_v, big_sem.at[1]).wait()
        attended = jnp.sum(p3_v[...].astype(F32), axis=0)
        hidden = res_v[...].astype(F32) + attended
        hid_v[...] = hidden
        ag_v[a, yc, g, l, c] = (hidden * gain_v[pl.ds(a * 7 + yc, 1), :]).astype(BF16)

    @when(jnp.logical_not(has_tile))
    def _():
        loads[3].wait()

    own = ag_v.at[a, yc, g, l, c]
    for d in FAR8:
        sends.go(own, own, g_sem.at[d - 1], ydev(d), even, has_tile)
    for d in FAR8:
        sends.go(own, own, g_sem.at[7 + d - 1], zdev(d), odd, first, has_tile)
    for d in FAR4:
        sends.go(own, own, g_sem.at[14 + d - 1], xdev(d), odd, second, has_tile)

    def hidden_copy(i):
        to_e = c * 16 + i
        far = remote(
            f_v.at[i], o_v.at[l, yc], loop_sems.at[i], big_sem.at[2], {"exp": to_e}
        )
        return to_e == e, far

    def hidden_go(i, carry):
        mine, far = hidden_copy(i)

        @when(mine)
        def _():
            pltpu.make_async_copy(f_v.at[i], o_v.at[l, yc], big_sem.at[2]).start()

        pl.when(jnp.logical_not(mine))(far.start)
        return carry

    def hidden_done(i, carry):
        mine, far = hidden_copy(i)
        pl.when(jnp.logical_not(mine))(far.wait_send)
        return carry

    @when(has_tile)
    def _():
        for i in range(16):
            f_v[i] = hid_v[i : i + 1, :]
        lax.fori_loop(0, 16, hidden_go, 0)

    @when(odd & second & has_tile)
    def _():
        for d in NEAR4:
            arrived(ag_v.at[xi(-d), yc, g, 1, 1], g_sem.at[14 + d - 1])

    for d in FAR8:
        blk = ag_v.at[:, yc, g, 1, 1]
        sends.go(blk, blk, g_sem.at[27 + d - 1], ydev(d), odd, second, has_tile)

    @when(even)
    def _():
        for d in NEAR8:

            @when(yi(-d) < 7)
            def _():
                arrived(ag_v.at[a, jnp.minimum(yi(-d), 6), g, 0, c], g_sem.at[d - 1])

    for d in FAR8:
        blk = ag_v.at[a, :, g, 0, c]
        sends.go(blk, blk, g_sem.at[17 + d - 1], zdev(d), even)

    @when(first & has_tile)
    def _():
        for d in NEAR8:

            @when(zi(-d) % 2 == 1)
            def _():
                arrived(ag_v.at[a, yc, zi(-d) // 2, 1, 0], g_sem.at[7 + d - 1])

    for d in FAR4:
        blk = ag_v.at[a, yc, :, 1, 0]
        sends.go(blk, blk, g_sem.at[24 + d - 1], xdev(d), first, has_tile)

    def part(p):
        offset = (0, 2, 6, 4)[p] + l * (1, 5, -3, 1)[p]
        return offset, (z - offset + 8) % 8 // 2

    def pass_on(p):
        offset, from_g = part(p)
        blk = ag_v.at[a, :, from_g, 0, c]
        if p == 0:

            @when(odd)
            def _():
                arrived(blk, g_sem.at[16 + jnp.maximum(offset, 1)])

        else:
            arrived(blk, g_sem.at[16 + offset])
        for d in FAR4:
            sends.go(blk, blk, g_sem.at[34 + (d - 1) * 4 + p], xdev(d))
        sends.go(blk, blk, core_sem.at[p], core_dev)

    pass_on(0)

    @when(first & has_tile)
    def _():
        for d in NEAR4:
            arrived(ag_v.at[xi(-d), yc, :, 1, 0], g_sem.at[24 + d - 1])

    blk_y = ag_v.at[:, yc, :, 1, 0]
    for d in FAR8:
        sends.go(blk_y, blk_y, g_sem.at[46 + d - 1], ydev(d), first, has_tile)
    sends.go(blk_y, blk_y, core_sem.at[16], core_dev, first, has_tile)

    @when(odd & second)
    def _():
        for d in NEAR8:

            @when(yi(-d) < 7)
            def _():
                arrived(ag_v.at[:, jnp.minimum(yi(-d), 6), g, 1, 1], g_sem.at[27 + d - 1])

    blk_z = ag_v.at[:, :, g, 1, 1]
    for d in FAR8:
        sends.go(blk_z, blk_z, g_sem.at[53 + d - 1], zdev(d), odd, second)
    sends.go(blk_z, blk_z, core_sem.at[24], core_dev, odd, second)

    pass_on(1)
    pass_on(2)
    pass_on(3)

    for p in range(4):
        from_g = part(p)[1]
        for d in NEAR4:
            blk = ag_v.at[xi(-d), :, from_g, 0, c]
            arrived(blk, g_sem.at[34 + (d - 1) * 4 + p])
            sends.go(blk, blk, core_sem.at[4 + (d - 1) * 4 + p], core_dev)
    for d in NEAR8:
        cond = first & (yi(-d) < 7)
        blk = ag_v.at[:, jnp.minimum(yi(-d), 6), :, 1, 0]

        @when(cond)
        def _():
            arrived(blk, g_sem.at[46 + d - 1])

        sends.go(blk, blk, core_sem.at[16 + d], core_dev, cond)
        cond = second & (zi(-d) % 2 == 1)
        blk = ag_v.at[:, :, zi(-d) // 2, 1, 1]

        @when(cond)
        def _():
            arrived(blk, g_sem.at[53 + d - 1])

        sends.go(blk, blk, core_sem.at[24 + d], core_dev, cond)
    for p in range(4):
        from_g = part(p)[1]
        arrived(ag_v.at[a, :, from_g, 0, 1 - c], core_sem.at[p])
        for d in NEAR4:
            arrived(
                ag_v.at[xi(-d), :, from_g, 0, 1 - c], core_sem.at[4 + (d - 1) * 4 + p]
            )
    for d in (0,) + NEAR8:

        @when(second & (yi(-d) < 7))
        def _():
            arrived(ag_v.at[:, jnp.minimum(yi(-d), 6), :, 1, 0], core_sem.at[16 + d])

        @when(first & (zi(-d) % 2 == 1))
        def _():
            arrived(ag_v.at[:, :, zi(-d) // 2, 1, 1], core_sem.at[24 + d])

    loads[7].wait()
    loads[8].wait()
    loads[9].wait()
    pieces = [ag_v[i // 7, i % 7].reshape(256, 128) for i in range(28)]
    square = jnp.zeros((256, 128), F32)
    for i in range(28):
        item = pieces[i].astype(F32) / gain_v[i : i + 1, :]
        square = square + item * item
    inverse = lax.rsqrt(jnp.sum(square, axis=1, keepdims=True) * (1.0 / 3584) + 1e-6)
    both = jnp.dot(jnp.concatenate(pieces, axis=1), wgu_v[...], preferred_element_type=F32)
    both = both * inverse
    gate = both[:, 0:128]
    act = gate / (1.0 + jnp.exp(-gate)) * both[:, 128:256] * rw_v[...]
    act = jnp.concatenate(
        [
            act[grp * 64 + mb * 32 : grp * 64 + mb * 32 + 32]
            for mb in range(2)
            for grp in range(4)
        ],
        axis=0,
    ).astype(BF16)
    for n, d in enumerate((2, 1, 3, 0)):
        x = xi(d)
        down = jnp.dot(
            act,
            wd_v[:, pl.ds(pl.multiple_of(x * 896, 128), 896)],
            preferred_element_type=F32,
        )
        for mb in range(2):
            for k in range(7):
                unit_v[n % 2, :, mb * 7 + k, :] = down[
                    mb * 128 : (mb + 1) * 128, k * 128 : (k + 1) * 128
                ]
        pd_v[x] = unit_v[n % 2].astype(BF16).reshape(4, 2, 8, 2, 16, 128)
        sends.go(pd_v.at[x, :, :, :, 1 - c], r0_v.at[x], r_sem.at[d], core_dev)

    def target(p):
        offset = (4, 2, 6, 0)[p] + l * (-1, 3, -5, 7)[p]
        return offset, (z + offset) % 8 // 2

    for d in (2, 1, 3, 0):
        x = xi(d)
        arrived(r0_v.at[x], r_sem.at[d])
        qs_v[x] = (pd_v[x, :, :, :, c].astype(F32) + r0_v[x].astype(F32)).astype(BF16)
        if d > 0:
            for p in range(4):
                sends.go(
                    qs_v.at[x, target(p)[1], 0],
                    r1x_v.at[d - 1, p],
                    r_sem.at[4 + (d - 1) * 4 + p],
                    xdev(d),
                )
    for d in FAR8:
        sends.go(
            qs_v.at[:, :, 1, yi(d)], r1y_v.at[d - 1], r_sem.at[16 + d - 1], ydev(d), first
        )
    for d in FAR8:
        sends.go(
            qs_v.at[:, zi(d) // 2, 1],
            r1z_v.at[d - 1],
            r_sem.at[23 + d - 1],
            zdev(d),
            second,
            zi(d) % 2 == 1,
        )

    def total_of(own_block, ref, count):
        result = own_block.astype(F32)
        for i in range(count):
            result = result + ref[i].astype(F32)
        return result

    def all_arrived(ref, base, count):
        for i in range(count):
            arrived(ref.at[i], r_sem.at[base + i])

    for p in range(4):
        offset, to_g = target(p)
        result = qs_v[a, to_g, 0].astype(F32)
        for d in NEAR4:
            arrived(r1x_v.at[d - 1, p], r_sem.at[4 + (d - 1) * 4 + p])
            result = result + r1x_v[d - 1, p].astype(F32)
        s1x_v[p] = result.astype(BF16)
        device = {"grp": to_g, "exp": y * 2 + c}
        slot = jnp.maximum(offset - 1, 0)
        conds = (odd,) if p == 3 else ()
        sends.go(s1x_v.at[p], r2x_v.at[slot], r_sem.at[30 + slot], device, *conds)

    @when(first)
    def _():
        all_arrived(r1y_v, 16, 7)
        s1y_v[...] = total_of(qs_v[:, :, 1, y], r1y_v, 7).astype(BF16)

    for d in FAR4:
        sends.go(s1y_v.at[xi(d)], r2y_v.at[d - 1], r_sem.at[37 + d - 1], xdev(d), first)

    @when(second & odd)
    def _():
        all_arrived(r1z_v, 23, 7)
        s1z_v[...] = total_of(qs_v[:, g, 1], r1z_v, 7).astype(BF16)

    for d in FAR8:
        sends.go(
            s1z_v.at[:, yi(d)], r2z_v.at[d - 1], r_sem.at[40 + d - 1], ydev(d), second, odd
        )

    @when(first)
    def _():
        all_arrived(r2y_v, 37, 3)
        s2y_v[...] = total_of(s1y_v[a], r2y_v, 3).astype(BF16)

    for d in FAR8:
        sends.go(
            s2y_v.at[zi(d) // 2],
            r3_v.at[d - 1],
            r_sem.at[47 + d - 1],
            zdev(d),
            first,
            zi(d) % 2 == 1,
        )

    @when(even)
    def _():
        all_arrived(r2x_v, 30, 7)
        s2x_v[...] = total_of(s1x_v[3], r2x_v, 7).astype(BF16)

    for d in FAR8:
        sends.go(s2x_v.at[yi(d)], r3_v.at[d - 1], r_sem.at[47 + d - 1], ydev(d), even)

    @when(second & odd)
    def _():
        all_arrived(r2z_v, 40, 7)
        s2z_v[...] = total_of(s1z_v[:, y], r2z_v, 7).astype(BF16)

    for d in FAR4:
        sends.go(s2z_v.at[xi(d)], r3_v.at[d - 1], r_sem.at[47 + d - 1], xdev(d), second, odd)

    pltpu.make_async_copy(o_v, o_v, big_sem.at[2]).wait()
    sends.drain()

    @when(has_tile)
    def _():
        lax.fori_loop(0, 16, hidden_done, 0)

    @when(even)
    def _():
        all_arrived(r3_v, 47, 7)
        fin_v[...] = total_of(s2x_v[y], r3_v, 7)

    @when(odd & first)
    def _():
        all_arrived(r3_v, 47, 7)
        fin_v[...] = total_of(s2y_v[g], r3_v, 7)

    @when(odd & second)
    def _():
        all_arrived(r3_v, 47, 3)
        fin_v[...] = total_of(s2z_v[a], r3_v, 3)

    rows = [
        jnp.concatenate(
            [fin_v[mb * 7 + k : mb * 7 + k + 1, :] + o_v[mb, k] for k in range(7)], axis=1
        )
        for mb in range(2)
    ]
    out_ref[...] = jnp.concatenate(rows, axis=0).astype(BF16)


def body(
    resid,
    queries,
    cache,
    lengths,
    w_value,
    w_out,
    norm_gain,
    route_ids,
    route_weights,
    w_gate,
    w_up,
    w_down,
):
    hbm = pl.BlockSpec(memory_space=pl.ANY)
    vmem = pl.BlockSpec(memory_space=pltpu.VMEM)
    smem = pl.BlockSpec(memory_space=pltpu.SMEM)

    def bf(*shape):
        return pltpu.VMEM(shape, BF16)

    def f32(*shape):
        return pltpu.VMEM(shape, F32)

    def dma(count):
        return pltpu.SemaphoreType.DMA((count,))

    return pl.pallas_call(
        kernel,
        out_shape=jax.ShapeDtypeStruct((2, 896), BF16),
        in_specs=[smem, vmem] + [hbm] * 10,
        out_specs=vmem,
        scratch_shapes=[
            bf(2, 64, 576),
            bf(2, 576, 512),
            bf(16, 128),
            pltpu.VMEM((2, 8, 128), jnp.int32),
            f32(2, 8, 128),
            bf(4, 2, 32, 512),
            bf(4, 2, 32, 896),
            bf(3584, 256),
            bf(128, 3584),
            f32(256, 128),
            f32(28, 128),
            bf(4, 2, 16, 640),
            bf(3, 2, 16, 640),
            f32(16, 8, 128),
            bf(8, 16, 128),
            bf(32, 16, 128),
            f32(32, 16, 128),
            bf(7, 4, 16, 128),
            bf(32, 16, 128),
            f32(16, 128),
            bf(4, 7, 4, 2, 2, 16, 128),
            bf(4, 4, 2, 8, 2, 16, 128),
            bf(4, 4, 2, 8, 16, 128),
            bf(4, 4, 2, 8, 16, 128),
            bf(3, 4, 8, 16, 128),
            bf(7, 4, 4, 16, 128),
            bf(7, 4, 8, 16, 128),
            bf(4, 8, 16, 128),
            bf(4, 4, 16, 128),
            bf(4, 8, 16, 128),
            bf(7, 8, 16, 128),
            bf(3, 4, 16, 128),
            bf(7, 4, 16, 128),
            bf(8, 16, 128),
            bf(4, 16, 128),
            bf(4, 16, 128),
            bf(7, 16, 128),
            f32(16, 1, 128),
            f32(2, 7, 1, 128),
            f32(2, 128, 16, 128),
            f32(16, 128),
            dma(10),
            dma(SEND_SEMS),
            dma(16),
            dma(6),
            dma(3),
            dma(3),
            dma(60),
            dma(32),
            dma(54),
        ],
        compiler_params=pltpu.CompilerParams(
            collective_id=0, has_side_effects=True, vmem_limit_bytes=56 * 1024 * 1024
        ),
        name="layer",
    )(
        lengths.reshape(1, 2),
        norm_gain.reshape(28, 128),
        queries[:, 0],
        jnp.swapaxes(cache[:, 0], 1, 2),
        resid,
        jnp.swapaxes(route_ids, 1, 2),
        jnp.swapaxes(route_weights, 1, 2),
        jnp.swapaxes(w_value, 1, 2),
        w_out,
        w_gate[0],
        w_up[0],
        w_down[0],
    ).reshape(2, 1, 896)


def solution(mesh):
    return jax.shard_map(
        body,
        mesh=mesh,
        in_specs=(
            P(None, "grp", None),
            P(None, ("grp", "exp"), None, None),
            P(None, ("grp", "exp"), "attn", None),
            P(None, ("grp", "exp")),
            P("exp", None, "attn"),
            P("exp", "attn", None),
            P(),
            P(),
            P(),
            P("exp", None, ("attn", "grp")),
            P("exp", None, ("attn", "grp")),
            P("exp", ("attn", "grp"), None),
        ),
        out_specs=P(None, ("grp", "exp"), "attn"),
        check_vma=False,
    )
```

time: 102 us -> 83.1 us (0.81)
  Pallas kernels: 90.2 us -> 80.6 us
  local copies, waits for them, and re-layouts: 9.63 us -> 1.27 us
  other arithmetic: 1.3 us -> 0 us
    pallas_call x1, Pallas kernels: 90.2 us -> 80.6 us  [body(): pl.pallas_call(kernel, out_shape=jax.ShapeDtypeStruct((2, 896), BF16), in...]
    unnamed x5 -> x1, local copies, waits for them, and re-layouts: 8.36 us -> 1.27 us
    reshape x1 -> x0, other arithmetic: 1.3 us -> none  [body(): norm_gain.astype(F32).reshape(28, 128)]
    pallas_call x1 -> x0, local copies, waits for them, and re-layouts: 1.28 us -> none  [body(): pl.pallas_call(kernel, out_shape=jax.ShapeDtypeStruct((2, 1, 896), BF16),...]
where the time goes in v2:
time: 83.1 us; the launch traced here: 81.9 us
  Pallas kernels  80.6 us (97%)
  local copies, waits for them, and re-layouts  1.27 us (2%)
    pallas_call x1, Pallas kernels, body(): pl.pallas_call(kernel, out_shape=jax.ShapeDtypeStruct((2, 896), BF16), in...  80.6 us

profile of v2, /device:TPU:1, one launch (start us, length us, event | category | flops | bytes accessed | tf_op | source)
XLA Modules:
  0.0 81.9 jit_solution(1731155742847236715)
XLA Ops:
  0.0 80.6 %layer.1 = bf16[2,896]{1,0:T(2,128)(2,1)} custom-call(s32[1,2]{1,0:T(1,128)} %bitcast.23, bf16[28,128]{1,0:T(8,128)(2,1)} %bitcast.20, bf16[2,64,576]{2,1,0:T(8,128)(2,1)} %bitcast.17, bf16[2,576,512]{2,1,0:T(8,128)(2,1)} %bitcast.13, bf16[2,32,3584]{2,1,0:T(8,128)(2,1)} %resid_hbm.1, s32[2,8,128]{2,1,0:T(8,128)} %bitcast.21, f32[2,8,128]{2,1,0:T(8,128)} %bitcast.22, ...), custom_call_target="tpu_custom_call" | custom-call | tf_op jit(solution)/shard_map/layer/pallas_call | solution.py:694
  80.6 1.3 %copy.14 = bf16[2,1,896]{2,0,1:T(2,128)(2,1)} copy(bf16[2,1,896]{2,0,1:T(2,128)(2,1)} %bitcast.19) | data formatting | bytes 7168

commit v3 on v2

--- a/solution.py
+++ b/solution.py
@@ -58,8 +58,8 @@
 
 
 def kernel(
-    len_ref,
-    gain_ref,
+    len_hbm,
+    gain_hbm,
     q_hbm,
     cache_hbm,
     resid_hbm,
@@ -71,6 +71,8 @@
     wu_hbm,
     wd_hbm,
     out_ref,
+    len_v,
+    gain16_v,
     q_v,
     cache_v,
     res_v,
@@ -92,8 +94,6 @@
     p3_v,
     hid_v,
     ag_v,
-    pd_v,
-    r0_v,
     qs_v,
     r1x_v,
     r1y_v,
@@ -179,14 +179,16 @@
                     wo_hbm.at[:, :, pl.ds(pl.multiple_of(a * 896, 128), 896)],
                     wo_v.at[a],
                 ),
-                (wg_hbm, wgu_v.at[:, pl.ds(0, 128)]),
-                (wu_hbm, wgu_v.at[:, pl.ds(128, 128)]),
-                (wd_hbm, wd_v),
+                (wg_hbm, wgu_v.at[c, :, pl.ds(0, 128)]),
+                (wu_hbm, wgu_v.at[c, :, pl.ds(128, 128)]),
+                (wd_hbm, wd_v.at[c]),
+                (len_hbm, len_v),
+                (gain_hbm, gain16_v),
             ]
         )
     ]
-    for load in loads:
-        load.start()
+    for i in (1, 0, 10):
+        loads[i].start()
 
     barrier = pltpu.get_barrier_semaphore()
 
@@ -205,9 +207,13 @@
         greet(xdev(d))
     lax.fori_loop(1, 8, greet_plane, 0)
 
-    gain_v[...] = gain_ref[...].astype(F32)
-    unit_v[:, :, 8:16, :] = jnp.zeros((2, 128, 8, 128), F32)
-
+    for i in (11, 2, 3, 4, 5, 6, 7, 8, 9):
+        loads[i].start()
+    loads[11].wait()
+    gain_v[...] = gain16_v[...].astype(F32)
+    unit_v[:, :, 8:16, :] = jnp.zeros((2, 64, 8, 128), F32)
+
+    loads[10].wait()
     loads[0].wait()
     loads[1].wait()
     row = lax.broadcasted_iota(jnp.int32, (64, 64), 0)
@@ -219,7 +225,7 @@
     for mb in range(2):
         qp = jnp.dot(perm, q_v[mb], preferred_element_type=F32).astype(BF16)
         scores = jnp.dot(qp, cache_v[mb], preferred_element_type=F32) * SCALE
-        visible = pos < len_ref[0, mb]
+        visible = pos < len_v[0, mb]
         top = jnp.max(jnp.where(visible, scores, -1e30), axis=1, keepdims=True)
         top = top.astype(BF16).astype(F32)
         weights = jnp.where(visible, jnp.exp(scores - top), 0.0)
@@ -238,13 +244,16 @@
     loads[4].wait()
     loads[5].wait()
     for mb in range(2):
-        gate = jnp.sum(
-            jnp.where(ids_v[mb] == e, wts_v[mb], 0.0), axis=0, keepdims=True
-        )
-        gate = jnp.broadcast_to(gate, (128, 128)).T
-        for grp in range(4):
-            at = (grp * 2 + mb) * 32
-            rw_v[at : at + 32, :] = gate[grp * 32 : (grp + 1) * 32, :]
+        for s in range(2):
+            gate = jnp.sum(
+                jnp.where(ids_v[mb] == e - c + s, wts_v[mb], 0.0), axis=0, keepdims=True
+            )
+            gate = jnp.broadcast_to(gate, (128, 128)).T
+            for grp in range(4):
+                at = grp * 32
+                rw_v[s, mb * 64 + grp * 16 : mb * 64 + grp * 16 + 16, :] = jnp.where(
+                    first, gate[at : at + 16, :], gate[at + 16 : at + 32, :]
+                )
 
     loads[2].wait()
     for d in FAR4:
@@ -325,6 +334,14 @@
                 device = {"exp": to_l * 16 + yi(d) * 2 + to_c}
                 sends.go(src, p3_v.at[e], big_sem.at[1], device, yi(d) < 7)
 
+    halves = [
+        (wg_hbm, wgu_v.at[c, :, pl.ds(0, 128)], wgu_v.at[1 - c, :, pl.ds(0, 128)]),
+        (wu_hbm, wgu_v.at[c, :, pl.ds(128, 128)], wgu_v.at[1 - c, :, pl.ds(128, 128)]),
+        (wd_hbm, wd_v.at[c], wd_v.at[1 - c]),
+    ]
+    for i, (src, dst, _) in enumerate(halves):
+        sends.go(src, dst, core_sem.at[i], core_dev)
+
     @when(has_tile)
     def _():
         pltpu.make_async_copy(s3_v.at[yc, l * 2 + c], p3_v.at[e], big_sem.at[1]).start()
@@ -333,13 +350,13 @@
         attended = jnp.sum(p3_v[...].astype(F32), axis=0)
         hidden = res_v[...].astype(F32) + attended
         hid_v[...] = hidden
-        ag_v[a, yc, g, l, c] = (hidden * gain_v[pl.ds(a * 7 + yc, 1), :]).astype(BF16)
+        ag_v[a, yc, l, g] = (hidden * gain_v[pl.ds(a * 7 + yc, 1), :]).astype(BF16)
 
     @when(jnp.logical_not(has_tile))
     def _():
         loads[3].wait()
 
-    own = ag_v.at[a, yc, g, l, c]
+    own = ag_v.at[a, yc, l, g]
     for d in FAR8:
         sends.go(own, own, g_sem.at[d - 1], ydev(d), even, has_tile)
     for d in FAR8:
@@ -378,10 +395,10 @@
     @when(odd & second & has_tile)
     def _():
         for d in NEAR4:
-            arrived(ag_v.at[xi(-d), yc, g, 1, 1], g_sem.at[14 + d - 1])
-
-    for d in FAR8:
-        blk = ag_v.at[:, yc, g, 1, 1]
+            arrived(ag_v.at[xi(-d), yc, 1, g], g_sem.at[14 + d - 1])
+
+    for d in FAR8:
+        blk = ag_v.at[:, yc, 1, g]
         sends.go(blk, blk, g_sem.at[27 + d - 1], ydev(d), odd, second, has_tile)
 
     @when(even)
@@ -390,10 +407,10 @@
 
             @when(yi(-d) < 7)
             def _():
-                arrived(ag_v.at[a, jnp.minimum(yi(-d), 6), g, 0, c], g_sem.at[d - 1])
-
-    for d in FAR8:
-        blk = ag_v.at[a, :, g, 0, c]
+                arrived(ag_v.at[a, jnp.minimum(yi(-d), 6), 0, g], g_sem.at[d - 1])
+
+    for d in FAR8:
+        blk = ag_v.at[a, :, 0, g]
         sends.go(blk, blk, g_sem.at[17 + d - 1], zdev(d), even)
 
     @when(first & has_tile)
@@ -402,10 +419,10 @@
 
             @when(zi(-d) % 2 == 1)
             def _():
-                arrived(ag_v.at[a, yc, zi(-d) // 2, 1, 0], g_sem.at[7 + d - 1])
+                arrived(ag_v.at[a, yc, 1, zi(-d) // 2], g_sem.at[7 + d - 1])
 
     for d in FAR4:
-        blk = ag_v.at[a, yc, :, 1, 0]
+        blk = ag_v.at[a, yc, 1]
         sends.go(blk, blk, g_sem.at[24 + d - 1], xdev(d), first, has_tile)
 
     def part(p):
@@ -414,7 +431,7 @@
 
     def pass_on(p):
         offset, from_g = part(p)
-        blk = ag_v.at[a, :, from_g, 0, c]
+        blk = ag_v.at[a, :, 0, from_g]
         if p == 0:
 
             @when(odd)
@@ -425,19 +442,17 @@
             arrived(blk, g_sem.at[16 + offset])
         for d in FAR4:
             sends.go(blk, blk, g_sem.at[34 + (d - 1) * 4 + p], xdev(d))
-        sends.go(blk, blk, core_sem.at[p], core_dev)
 
     pass_on(0)
 
     @when(first & has_tile)
     def _():
         for d in NEAR4:
-            arrived(ag_v.at[xi(-d), yc, :, 1, 0], g_sem.at[24 + d - 1])
-
-    blk_y = ag_v.at[:, yc, :, 1, 0]
+            arrived(ag_v.at[xi(-d), yc, 1], g_sem.at[24 + d - 1])
+
+    blk_y = ag_v.at[:, yc, 1]
     for d in FAR8:
         sends.go(blk_y, blk_y, g_sem.at[46 + d - 1], ydev(d), first, has_tile)
-    sends.go(blk_y, blk_y, core_sem.at[16], core_dev, first, has_tile)
 
     @when(odd & second)
     def _():
@@ -445,12 +460,11 @@
 
             @when(yi(-d) < 7)
             def _():
-                arrived(ag_v.at[:, jnp.minimum(yi(-d), 6), g, 1, 1], g_sem.at[27 + d - 1])
-
-    blk_z = ag_v.at[:, :, g, 1, 1]
+                arrived(ag_v.at[:, jnp.minimum(yi(-d), 6), 1, g], g_sem.at[27 + d - 1])
+
+    blk_z = ag_v.at[:, :, 1, g]
     for d in FAR8:
         sends.go(blk_z, blk_z, g_sem.at[53 + d - 1], zdev(d), odd, second)
-    sends.go(blk_z, blk_z, core_sem.at[24], core_dev, odd, second)
 
     pass_on(1)
     pass_on(2)
@@ -459,179 +473,139 @@
     for p in range(4):
         from_g = part(p)[1]
         for d in NEAR4:
-            blk = ag_v.at[xi(-d), :, from_g, 0, c]
-            arrived(blk, g_sem.at[34 + (d - 1) * 4 + p])
-            sends.go(blk, blk, core_sem.at[4 + (d - 1) * 4 + p], core_dev)
+            arrived(ag_v.at[xi(-d), :, 0, from_g], g_sem.at[34 + (d - 1) * 4 + p])
     for d in NEAR8:
-        cond = first & (yi(-d) < 7)
-        blk = ag_v.at[:, jnp.minimum(yi(-d), 6), :, 1, 0]
-
-        @when(cond)
+
+        @when(first & (yi(-d) < 7))
         def _():
-            arrived(blk, g_sem.at[46 + d - 1])
-
-        sends.go(blk, blk, core_sem.at[16 + d], core_dev, cond)
-        cond = second & (zi(-d) % 2 == 1)
-        blk = ag_v.at[:, :, zi(-d) // 2, 1, 1]
-
-        @when(cond)
+            arrived(ag_v.at[:, jnp.minimum(yi(-d), 6), 1], g_sem.at[46 + d - 1])
+
+        @when(second & (zi(-d) % 2 == 1))
         def _():
-            arrived(blk, g_sem.at[53 + d - 1])
-
-        sends.go(blk, blk, core_sem.at[24 + d], core_dev, cond)
-    for p in range(4):
-        from_g = part(p)[1]
-        arrived(ag_v.at[a, :, from_g, 0, 1 - c], core_sem.at[p])
-        for d in NEAR4:
-            arrived(
-                ag_v.at[xi(-d), :, from_g, 0, 1 - c], core_sem.at[4 + (d - 1) * 4 + p]
-            )
-    for d in (0,) + NEAR8:
-
-        @when(second & (yi(-d) < 7))
-        def _():
-            arrived(ag_v.at[:, jnp.minimum(yi(-d), 6), :, 1, 0], core_sem.at[16 + d])
-
-        @when(first & (zi(-d) % 2 == 1))
-        def _():
-            arrived(ag_v.at[:, :, zi(-d) // 2, 1, 1], core_sem.at[24 + d])
+            arrived(ag_v.at[:, :, 1, zi(-d) // 2], g_sem.at[53 + d - 1])
 
     loads[7].wait()
     loads[8].wait()
     loads[9].wait()
-    pieces = [ag_v[i // 7, i % 7].reshape(256, 128) for i in range(28)]
-    square = jnp.zeros((256, 128), F32)
+    for i, (_, _, dst) in enumerate(halves):
+        arrived(dst, core_sem.at[i])
+    pieces = [ag_v[i // 7, i % 7].reshape(128, 128) for i in range(28)]
+    square = jnp.zeros((128, 128), F32)
     for i in range(28):
         item = pieces[i].astype(F32) / gain_v[i : i + 1, :]
         square = square + item * item
     inverse = lax.rsqrt(jnp.sum(square, axis=1, keepdims=True) * (1.0 / 3584) + 1e-6)
-    both = jnp.dot(jnp.concatenate(pieces, axis=1), wgu_v[...], preferred_element_type=F32)
-    both = both * inverse
-    gate = both[:, 0:128]
-    act = gate / (1.0 + jnp.exp(-gate)) * both[:, 128:256] * rw_v[...]
-    act = jnp.concatenate(
-        [
-            act[grp * 64 + mb * 32 : grp * 64 + mb * 32 + 32]
-            for mb in range(2)
-            for grp in range(4)
-        ],
-        axis=0,
-    ).astype(BF16)
+    rows = jnp.concatenate(pieces, axis=1)
+    acts = []
+    for s in range(2):
+        both = jnp.dot(rows, wgu_v[s], preferred_element_type=F32) * inverse
+        gate = both[:, 0:128]
+        acts.append(gate / (1.0 + jnp.exp(-gate)) * both[:, 128:256] * rw_v[s])
+    act = jnp.concatenate(acts, axis=1).astype(BF16)
+    def target(p):
+        offset = (4, 2, 6, 0)[p] + (l + c) % 2 * (-1, 3, -5, 7)[p]
+        return offset, (z + offset) % 8 // 2
+
     for n, d in enumerate((2, 1, 3, 0)):
         x = xi(d)
         down = jnp.dot(
             act,
-            wd_v[:, pl.ds(pl.multiple_of(x * 896, 128), 896)],
+            wd_v[:, :, pl.ds(pl.multiple_of(x * 896, 128), 896)].reshape(256, 896),
             preferred_element_type=F32,
         )
         for mb in range(2):
             for k in range(7):
                 unit_v[n % 2, :, mb * 7 + k, :] = down[
-                    mb * 128 : (mb + 1) * 128, k * 128 : (k + 1) * 128
+                    mb * 64 : (mb + 1) * 64, k * 128 : (k + 1) * 128
                 ]
-        pd_v[x] = unit_v[n % 2].astype(BF16).reshape(4, 2, 8, 2, 16, 128)
-        sends.go(pd_v.at[x, :, :, :, 1 - c], r0_v.at[x], r_sem.at[d], core_dev)
-
-    def target(p):
-        offset = (4, 2, 6, 0)[p] + l * (-1, 3, -5, 7)[p]
-        return offset, (z + offset) % 8 // 2
-
-    for d in (2, 1, 3, 0):
-        x = xi(d)
-        arrived(r0_v.at[x], r_sem.at[d])
-        qs_v[x] = (pd_v[x, :, :, :, c].astype(F32) + r0_v[x].astype(F32)).astype(BF16)
+        qs_v[x] = unit_v[n % 2].astype(BF16).reshape(4, 8, 2, 16, 128)
         if d > 0:
             for p in range(4):
                 sends.go(
-                    qs_v.at[x, target(p)[1], 0],
+                    qs_v.at[x, target(p)[1], :, 0],
                     r1x_v.at[d - 1, p],
-                    r_sem.at[4 + (d - 1) * 4 + p],
+                    r_sem.at[(d - 1) * 4 + p],
                     xdev(d),
                 )
+
     for d in FAR8:
         sends.go(
-            qs_v.at[:, :, 1, yi(d)], r1y_v.at[d - 1], r_sem.at[16 + d - 1], ydev(d), first
+            qs_v.at[:, :, yi(d), 1], r1y_v.at[d - 1], r_sem.at[12 + d - 1], ydev(d), first
         )
     for d in FAR8:
         sends.go(
-            qs_v.at[:, zi(d) // 2, 1],
+            qs_v.at[:, zi(d) // 2, :, 1],
             r1z_v.at[d - 1],
-            r_sem.at[23 + d - 1],
+            r_sem.at[19 + d - 1],
             zdev(d),
             second,
             zi(d) % 2 == 1,
         )
 
-    def total_of(own_block, ref, count):
-        result = own_block.astype(F32)
-        for i in range(count):
-            result = result + ref[i].astype(F32)
+    def total_of(blocks):
+        result = blocks[0].astype(F32)
+        for blk in blocks[1:]:
+            result = result + blk.astype(F32)
         return result
 
-    def all_arrived(ref, base, count):
-        for i in range(count):
+    def take(ref, base, items):
+        for i in items:
             arrived(ref.at[i], r_sem.at[base + i])
+        return [ref[i] for i in items]
 
     for p in range(4):
         offset, to_g = target(p)
-        result = qs_v[a, to_g, 0].astype(F32)
+        result = qs_v[a, to_g, :, 0].astype(F32)
         for d in NEAR4:
-            arrived(r1x_v.at[d - 1, p], r_sem.at[4 + (d - 1) * 4 + p])
+            arrived(r1x_v.at[d - 1, p], r_sem.at[(d - 1) * 4 + p])
             result = result + r1x_v[d - 1, p].astype(F32)
         s1x_v[p] = result.astype(BF16)
-        device = {"grp": to_g, "exp": y * 2 + c}
+        device = {"grp": to_g, "exp": c * 16 + y * 2 + c}
         slot = jnp.maximum(offset - 1, 0)
-        conds = (odd,) if p == 3 else ()
-        sends.go(s1x_v.at[p], r2x_v.at[slot], r_sem.at[30 + slot], device, *conds)
+        conds = (l != c,) if p == 3 else ()
+        sends.go(s1x_v.at[p], r2x_v.at[slot], r_sem.at[26 + slot], device, *conds)
 
     @when(first)
     def _():
-        all_arrived(r1y_v, 16, 7)
-        s1y_v[...] = total_of(qs_v[:, :, 1, y], r1y_v, 7).astype(BF16)
+        s1y_v[...] = total_of([qs_v[:, :, y, 1]] + take(r1y_v, 12, range(7))).astype(BF16)
 
     for d in FAR4:
-        sends.go(s1y_v.at[xi(d)], r2y_v.at[d - 1], r_sem.at[37 + d - 1], xdev(d), first)
+        sends.go(s1y_v.at[xi(d)], r2y_v.at[d - 1], r_sem.at[33 + d - 1], xdev(d), first)
 
     @when(second & odd)
     def _():
-        all_arrived(r1z_v, 23, 7)
-        s1z_v[...] = total_of(qs_v[:, g, 1], r1z_v, 7).astype(BF16)
+        s1z_v[...] = total_of([qs_v[:, g, :, 1]] + take(r1z_v, 19, range(7))).astype(BF16)
 
     for d in FAR8:
         sends.go(
-            s1z_v.at[:, yi(d)], r2z_v.at[d - 1], r_sem.at[40 + d - 1], ydev(d), second, odd
+            s1z_v.at[:, yi(d)], r2z_v.at[d - 1], r_sem.at[36 + d - 1], ydev(d), second, odd
         )
 
     @when(first)
     def _():
-        all_arrived(r2y_v, 37, 3)
-        s2y_v[...] = total_of(s1y_v[a], r2y_v, 3).astype(BF16)
-
-    for d in FAR8:
+        s2y_v[...] = total_of([s1y_v[a]] + take(r2y_v, 33, range(3))).astype(BF16)
+
+    for d in FAR8 + (0,):
+        device = {"grp": zi(d) // 2, "exp": y * 2 + 1}
         sends.go(
-            s2y_v.at[zi(d) // 2],
-            r3_v.at[d - 1],
-            r_sem.at[47 + d - 1],
-            zdev(d),
-            first,
-            zi(d) % 2 == 1,
-        )
-
-    @when(even)
-    def _():
-        all_arrived(r2x_v, 30, 7)
-        s2x_v[...] = total_of(s1x_v[3], r2x_v, 7).astype(BF16)
-
-    for d in FAR8:
-        sends.go(s2x_v.at[yi(d)], r3_v.at[d - 1], r_sem.at[47 + d - 1], ydev(d), even)
+            s2y_v.at[zi(d) // 2], r3_v.at[d], r_sem.at[43 + d], device, first, zi(d) % 2 == 0
+        )
+
+    @when(l == c)
+    def _():
+        s2x_v[...] = total_of([s1x_v[3]] + take(r2x_v, 26, range(7))).astype(BF16)
+
+    for d in FAR8 + (0,):
+        device = {"exp": l * 16 + yi(d) * 2}
+        conds = (l == c, second) if d == 0 else (l == c,)
+        sends.go(s2x_v.at[yi(d)], r3_v.at[d], r_sem.at[43 + d], device, *conds)
 
     @when(second & odd)
     def _():
-        all_arrived(r2z_v, 40, 7)
-        s2z_v[...] = total_of(s1z_v[:, y], r2z_v, 7).astype(BF16)
+        s2z_v[...] = total_of([s1z_v[:, y]] + take(r2z_v, 36, range(7))).astype(BF16)
 
     for d in FAR4:
-        sends.go(s2z_v.at[xi(d)], r3_v.at[d - 1], r_sem.at[47 + d - 1], xdev(d), second, odd)
+        sends.go(s2z_v.at[xi(d)], r3_v.at[d], r_sem.at[43 + d], xdev(d), second, odd)
 
     pltpu.make_async_copy(o_v, o_v, big_sem.at[2]).wait()
     sends.drain()
@@ -640,20 +614,17 @@
     def _():
         lax.fori_loop(0, 16, hidden_done, 0)
 
-    @when(even)
-    def _():
-        all_arrived(r3_v, 47, 7)
-        fin_v[...] = total_of(s2x_v[y], r3_v, 7)
-
-    @when(odd & first)
-    def _():
-        all_arrived(r3_v, 47, 7)
-        fin_v[...] = total_of(s2y_v[g], r3_v, 7)
+    @when(even & first)
+    def _():
+        fin_v[...] = total_of([s2x_v[y]] + take(r3_v, 43, range(1, 8)))
+
+    @when(l != c)
+    def _():
+        fin_v[...] = total_of(take(r3_v, 43, range(8)))
 
     @when(odd & second)
     def _():
-        all_arrived(r3_v, 47, 3)
-        fin_v[...] = total_of(s2z_v[a], r3_v, 3)
+        fin_v[...] = total_of([s2z_v[a]] + take(r3_v, 43, range(1, 4)))
 
     rows = [
         jnp.concatenate(
@@ -680,7 +651,6 @@
 ):
     hbm = pl.BlockSpec(memory_space=pl.ANY)
     vmem = pl.BlockSpec(memory_space=pltpu.VMEM)
-    smem = pl.BlockSpec(memory_space=pltpu.SMEM)
 
     def bf(*shape):
         return pltpu.VMEM(shape, BF16)
@@ -694,9 +664,11 @@
     return pl.pallas_call(
         kernel,
         out_shape=jax.ShapeDtypeStruct((2, 896), BF16),
-        in_specs=[smem, vmem] + [hbm] * 10,
+        in_specs=[hbm] * 12,
         out_specs=vmem,
         scratch_shapes=[
+            pltpu.SMEM((1, 2), jnp.int32),
+            bf(28, 128),
             bf(2, 64, 576),
             bf(2, 576, 512),
             bf(16, 128),
@@ -704,9 +676,9 @@
             f32(2, 8, 128),
             bf(4, 2, 32, 512),
             bf(4, 2, 32, 896),
-            bf(3584, 256),
-            bf(128, 3584),
-            f32(256, 128),
+            bf(2, 3584, 256),
+            bf(2, 128, 3584),
+            f32(2, 128, 128),
             f32(28, 128),
             bf(4, 2, 16, 640),
             bf(3, 2, 16, 640),
@@ -717,10 +689,8 @@
             bf(7, 4, 16, 128),
             bf(32, 16, 128),
             f32(16, 128),
-            bf(4, 7, 4, 2, 2, 16, 128),
-            bf(4, 4, 2, 8, 2, 16, 128),
-            bf(4, 4, 2, 8, 16, 128),
-            bf(4, 4, 2, 8, 16, 128),
+            bf(4, 7, 2, 4, 16, 128),
+            bf(4, 4, 8, 2, 16, 128),
             bf(3, 4, 8, 16, 128),
             bf(7, 4, 4, 16, 128),
             bf(7, 4, 8, 16, 128),
@@ -733,20 +703,20 @@
             bf(8, 16, 128),
             bf(4, 16, 128),
             bf(4, 16, 128),
-            bf(7, 16, 128),
+            bf(8, 16, 128),
             f32(16, 1, 128),
             f32(2, 7, 1, 128),
-            f32(2, 128, 16, 128),
+            f32(2, 64, 16, 128),
             f32(16, 128),
-            dma(10),
+            dma(12),
             dma(SEND_SEMS),
             dma(16),
             dma(6),
             dma(3),
             dma(3),
             dma(60),
-            dma(32),
-            dma(54),
+            dma(3),
+            dma(51),
         ],
         compiler_params=pltpu.CompilerParams(
             collective_id=0, has_side_effects=True, vmem_limit_bytes=56 * 1024 * 1024

time: 83.1 us -> 79.4 us (0.955); the launches traced: 81.9 us -> 79.2 us
  Pallas kernels: 80.6 us -> 77.9 us
    pallas_call x1, Pallas kernels: 80.6 us -> 77.9 us  [body(): pl.pallas_call(kernel, out_shape=jax.ShapeDtypeStruct((2, 896), BF16), in...]
where the time goes in v3:
time: 79.4 us; the launch traced here: 79.2 us
  Pallas kernels  77.9 us (98%)
  local copies, waits for them, and re-layouts  1.27 us (2%)
    pallas_call x1, Pallas kernels, body(): pl.pallas_call(kernel, out_shape=jax.ShapeDtypeStruct((2, 896), BF16), in...  77.9 us

profile of v3, /device:TPU:1, one launch (start us, length us, event | category | flops | bytes accessed | tf_op | source)
XLA Modules:
  0.0 79.2 jit_solution(9073113468864958853)
XLA Ops:
  0.0 77.9 %layer.1 = bf16[2,896]{1,0:T(2,128)(2,1)} custom-call(s32[1,2]{1,0:T(1,128)} %bitcast.23, bf16[28,128]{1,0:T(8,128)(2,1)} %bitcast.20, bf16[2,64,576]{2,1,0:T(8,128)(2,1)} %bitcast.17, bf16[2,576,512]{2,1,0:T(8,128)(2,1)} %bitcast.13, bf16[2,32,3584]{2,1,0:T(8,128)(2,1)} %resid_hbm.1, s32[2,8,128]{2,1,0:T(8,128)} %bitcast.21, f32[2,8,128]{2,1,0:T(8,128)} %bitcast.22, ...), custom_call_target="tpu_custom_call" | custom-call | tf_op jit(solution)/shard_map/layer/pallas_call | solution.py:664
  77.9 1.3 %copy.14 = bf16[2,1,896]{2,0,1:T(2,128)(2,1)} copy(bf16[2,1,896]{2,0,1:T(2,128)(2,1)} %bitcast.19) | data formatting | bytes 7168

commit v4 on v3

--- a/solution.py
+++ b/solution.py
@@ -52,9 +52,10 @@
 
 FAR8 = (4, 3, 5, 2, 6, 1, 7)
 FAR4 = (2, 1, 3)
+QUARTERS = (2, 1, 3, 0)
 NEAR8 = (1, 7, 2, 6, 3, 5, 4)
 NEAR4 = (1, 3, 2)
-SEND_SEMS = 232
+SEND_SEMS = 290
 
 
 def kernel(
@@ -506,7 +507,7 @@
         offset = (4, 2, 6, 0)[p] + (l + c) % 2 * (-1, 3, -5, 7)[p]
         return offset, (z + offset) % 8 // 2
 
-    for n, d in enumerate((2, 1, 3, 0)):
+    for n, d in enumerate(QUARTERS):
         x = xi(d)
         down = jnp.dot(
             act,
@@ -527,20 +528,22 @@
                     r_sem.at[(d - 1) * 4 + p],
                     xdev(d),
                 )
-
-    for d in FAR8:
-        sends.go(
-            qs_v.at[:, :, yi(d), 1], r1y_v.at[d - 1], r_sem.at[12 + d - 1], ydev(d), first
-        )
-    for d in FAR8:
-        sends.go(
-            qs_v.at[:, zi(d) // 2, :, 1],
-            r1z_v.at[d - 1],
-            r_sem.at[19 + d - 1],
-            zdev(d),
-            second,
-            zi(d) % 2 == 1,
-        )
+        for to in FAR8:
+            sends.go(
+                qs_v.at[x, :, yi(to), 1],
+                r1y_v.at[to - 1, n],
+                r_sem.at[12 + (to - 1) * 4 + n],
+                ydev(to),
+                first,
+            )
+            sends.go(
+                qs_v.at[x, zi(to) // 2, :, 1],
+                r1z_v.at[to - 1, n],
+                r_sem.at[40 + (to - 1) * 4 + n],
+                zdev(to),
+                second,
+                zi(to) % 2 == 1,
+            )
 
     def total_of(blocks):
         result = blocks[0].astype(F32)
@@ -563,49 +566,60 @@
         device = {"grp": to_g, "exp": c * 16 + y * 2 + c}
         slot = jnp.maximum(offset - 1, 0)
         conds = (l != c,) if p == 3 else ()
-        sends.go(s1x_v.at[p], r2x_v.at[slot], r_sem.at[26 + slot], device, *conds)
-
-    @when(first)
-    def _():
-        s1y_v[...] = total_of([qs_v[:, :, y, 1]] + take(r1y_v, 12, range(7))).astype(BF16)
-
-    for d in FAR4:
-        sends.go(s1y_v.at[xi(d)], r2y_v.at[d - 1], r_sem.at[33 + d - 1], xdev(d), first)
+        sends.go(s1x_v.at[p], r2x_v.at[slot], r_sem.at[68 + slot], device, *conds)
+
+        n, d = p, QUARTERS[p]
+
+        @when(first)
+        def _():
+            blocks = [qs_v[xi(d), :, y, 1]]
+            for i in range(7):
+                arrived(r1y_v.at[i, n], r_sem.at[12 + i * 4 + n])
+                blocks.append(r1y_v[i, n])
+            s1y_v[n] = total_of(blocks).astype(BF16)
+
+        if d > 0:
+            sends.go(s1y_v.at[n], r2y_v.at[d - 1], r_sem.at[75 + d - 1], xdev(d), first)
 
     @when(second & odd)
     def _():
-        s1z_v[...] = total_of([qs_v[:, g, :, 1]] + take(r1z_v, 19, range(7))).astype(BF16)
+        for n, d in enumerate(QUARTERS):
+            blocks = [qs_v[xi(d), g, :, 1]]
+            for i in range(7):
+                arrived(r1z_v.at[i, n], r_sem.at[40 + i * 4 + n])
+                blocks.append(r1z_v[i, n])
+            s1z_v[xi(d)] = total_of(blocks).astype(BF16)
 
     for d in FAR8:
         sends.go(
-            s1z_v.at[:, yi(d)], r2z_v.at[d - 1], r_sem.at[36 + d - 1], ydev(d), second, odd
+            s1z_v.at[:, yi(d)], r2z_v.at[d - 1], r_sem.at[78 + d - 1], ydev(d), second, odd
         )
 
     @when(first)
     def _():
-        s2y_v[...] = total_of([s1y_v[a]] + take(r2y_v, 33, range(3))).astype(BF16)
+        s2y_v[...] = total_of([s1y_v[3]] + take(r2y_v, 75, range(3))).astype(BF16)
 
     for d in FAR8 + (0,):
         device = {"grp": zi(d) // 2, "exp": y * 2 + 1}
         sends.go(
-            s2y_v.at[zi(d) // 2], r3_v.at[d], r_sem.at[43 + d], device, first, zi(d) % 2 == 0
+            s2y_v.at[zi(d) // 2], r3_v.at[d], r_sem.at[85 + d], device, first, zi(d) % 2 == 0
         )
 
     @when(l == c)
     def _():
-        s2x_v[...] = total_of([s1x_v[3]] + take(r2x_v, 26, range(7))).astype(BF16)
+        s2x_v[...] = total_of([s1x_v[3]] + take(r2x_v, 68, range(7))).astype(BF16)
 
     for d in FAR8 + (0,):
         device = {"exp": l * 16 + yi(d) * 2}
         conds = (l == c, second) if d == 0 else (l == c,)
-        sends.go(s2x_v.at[yi(d)], r3_v.at[d], r_sem.at[43 + d], device, *conds)
+        sends.go(s2x_v.at[yi(d)], r3_v.at[d], r_sem.at[85 + d], device, *conds)
 
     @when(second & odd)
     def _():
-        s2z_v[...] = total_of([s1z_v[:, y]] + take(r2z_v, 36, range(7))).astype(BF16)
+        s2z_v[...] = total_of([s1z_v[:, y]] + take(r2z_v, 78, range(7))).astype(BF16)
 
     for d in FAR4:
-        sends.go(s2z_v.at[xi(d)], r3_v.at[d], r_sem.at[43 + d], xdev(d), second, odd)
+        sends.go(s2z_v.at[xi(d)], r3_v.at[d], r_sem.at[85 + d], xdev(d), second, odd)
 
     pltpu.make_async_copy(o_v, o_v, big_sem.at[2]).wait()
     sends.drain()
@@ -616,15 +630,15 @@
 
     @when(even & first)
     def _():
-        fin_v[...] = total_of([s2x_v[y]] + take(r3_v, 43, range(1, 8)))
+        fin_v[...] = total_of([s2x_v[y]] + take(r3_v, 85, range(1, 8)))
 
     @when(l != c)
     def _():
-        fin_v[...] = total_of(take(r3_v, 43, range(8)))
+        fin_v[...] = total_of(take(r3_v, 85, range(8)))
 
     @when(odd & second)
     def _():
-        fin_v[...] = total_of([s2z_v[a]] + take(r3_v, 43, range(1, 4)))
+        fin_v[...] = total_of([s2z_v[a]] + take(r3_v, 85, range(1, 4)))
 
     rows = [
         jnp.concatenate(
@@ -716,7 +730,7 @@
             dma(3),
             dma(60),
             dma(3),
-            dma(51),
+            dma(93),
         ],
         compiler_params=pltpu.CompilerParams(
             collective_id=0, has_side_effects=True, vmem_limit_bytes=56 * 1024 * 1024

time: 79.4 us -> 77 us (0.970)
  Pallas kernels: 77.9 us -> 75.5 us
    pallas_call x1, Pallas kernels: 77.9 us -> 75.5 us  [body(): pl.pallas_call(kernel, out_shape=jax.ShapeDtypeStruct((2, 896), BF16), in...]
where the time goes in v4:
time: 77 us; the launch traced here: 76.8 us
  Pallas kernels  75.5 us (98%)
  local copies, waits for them, and re-layouts  1.27 us (2%)
    pallas_call x1, Pallas kernels, body(): pl.pallas_call(kernel, out_shape=jax.ShapeDtypeStruct((2, 896), BF16), in...  75.5 us

profile of v4, /device:TPU:1, one launch (start us, length us, event | category | flops | bytes accessed | tf_op | source)
XLA Modules:
  0.0 76.8 jit_solution(2956984196207460756)
XLA Ops:
  0.0 75.5 %layer.1 = bf16[2,896]{1,0:T(2,128)(2,1)} custom-call(s32[1,2]{1,0:T(1,128)} %bitcast.23, bf16[28,128]{1,0:T(8,128)(2,1)} %bitcast.20, bf16[2,64,576]{2,1,0:T(8,128)(2,1)} %bitcast.17, bf16[2,576,512]{2,1,0:T(8,128)(2,1)} %bitcast.13, bf16[2,32,3584]{2,1,0:T(8,128)(2,1)} %resid_hbm.1, s32[2,8,128]{2,1,0:T(8,128)} %bitcast.21, f32[2,8,128]{2,1,0:T(8,128)} %bitcast.22, ...), custom_call_target="tpu_custom_call" | custom-call | tf_op jit(solution)/shard_map/layer/pallas_call | solution.py:678
  75.5 1.3 %copy.14 = bf16[2,1,896]{2,0,1:T(2,128)(2,1)} copy(bf16[2,1,896]{2,0,1:T(2,128)(2,1)} %bitcast.19) | data formatting | bytes 7168

commit v5 on v4

--- a/solution.py
+++ b/solution.py
@@ -41,13 +41,14 @@
             pl.when(cond)(copy.start)
         self.pending.append((cond, copy))
 
-    def drain(self):
-        for cond, copy in self.pending:
+    def drain(self, count=None):
+        count = len(self.pending) if count is None else count
+        for cond, copy in self.pending[:count]:
             if cond is None:
                 copy.wait_send()
             else:
                 pl.when(cond)(copy.wait_send)
-        self.pending = []
+        self.pending = self.pending[count:]
 
 
 FAR8 = (4, 3, 5, 2, 6, 1, 7)
@@ -387,12 +388,6 @@
         pl.when(jnp.logical_not(mine))(far.wait_send)
         return carry
 
-    @when(has_tile)
-    def _():
-        for i in range(16):
-            f_v[i] = hid_v[i : i + 1, :]
-        lax.fori_loop(0, 16, hidden_go, 0)
-
     @when(odd & second & has_tile)
     def _():
         for d in NEAR4:
@@ -444,6 +439,7 @@
         for d in FAR4:
             sends.go(blk, blk, g_sem.at[34 + (d - 1) * 4 + p], xdev(d))
 
+    before = len(sends.pending)
     pass_on(0)
 
     @when(first & has_tile)
@@ -470,6 +466,13 @@
     pass_on(1)
     pass_on(2)
     pass_on(3)
+    @when(has_tile)
+    def _():
+        for i in range(16):
+            f_v[i] = hid_v[i : i + 1, :]
+        lax.fori_loop(0, 16, hidden_go, 0)
+
+    sends.drain(before)
 
     for p in range(4):
         from_g = part(p)[1]
@@ -507,6 +510,7 @@
         offset = (4, 2, 6, 0)[p] + (l + c) % 2 * (-1, 3, -5, 7)[p]
         return offset, (z + offset) % 8 // 2
 
+    before = len(sends.pending)
     for n, d in enumerate(QUARTERS):
         x = xi(d)
         down = jnp.dot(
@@ -545,6 +549,9 @@
                 zi(to) % 2 == 1,
             )
 
+    sends.drain(before)
+    before = len(sends.pending)
+
     def total_of(blocks):
         result = blocks[0].astype(F32)
         for blk in blocks[1:]:
@@ -568,7 +575,7 @@
         conds = (l != c,) if p == 3 else ()
         sends.go(s1x_v.at[p], r2x_v.at[slot], r_sem.at[68 + slot], device, *conds)
 
-        n, d = p, QUARTERS[p]
+    for n, d in enumerate(QUARTERS):
 
         @when(first)
         def _():
@@ -594,6 +601,7 @@
         sends.go(
             s1z_v.at[:, yi(d)], r2z_v.at[d - 1], r_sem.at[78 + d - 1], ydev(d), second, odd
         )
+    sends.drain(before)
 
     @when(first)
     def _():

time: 77 us -> 76.9 us (level)
  no operation moved by 1% of the time
where the time goes in v5:
time: 76.9 us; the launch traced here: 76.8 us
  Pallas kernels  75.5 us (98%)
  local copies, waits for them, and re-layouts  1.27 us (2%)
    pallas_call x1, Pallas kernels, body(): pl.pallas_call(kernel, out_shape=jax.ShapeDtypeStruct((2, 896), BF16), in...  75.5 us

profile of v5, /device:TPU:1, one launch (start us, length us, event | category | flops | bytes accessed | tf_op | source)
XLA Modules:
  0.0 76.8 jit_solution(18162652484789781656)
XLA Ops:
  0.0 75.5 %layer.1 = bf16[2,896]{1,0:T(2,128)(2,1)} custom-call(s32[1,2]{1,0:T(1,128)} %bitcast.23, bf16[28,128]{1,0:T(8,128)(2,1)} %bitcast.20, bf16[2,64,576]{2,1,0:T(8,128)(2,1)} %bitcast.17, bf16[2,576,512]{2,1,0:T(8,128)(2,1)} %bitcast.13, bf16[2,32,3584]{2,1,0:T(8,128)(2,1)} %resid_hbm.1, s32[2,8,128]{2,1,0:T(8,128)} %bitcast.21, f32[2,8,128]{2,1,0:T(8,128)} %bitcast.22, ...), custom_call_target="tpu_custom_call" | custom-call | tf_op jit(solution)/shard_map/layer/pallas_call | solution.py:686
  75.5 1.3 %copy.14 = bf16[2,1,896]{2,0,1:T(2,128)(2,1)} copy(bf16[2,1,896]{2,0,1:T(2,128)(2,1)} %bitcast.19) | data formatting | bytes 7168
